TPU v7x, 32 devices: a whole 2x2x4 slice. The times are simulated.
32 devices in a mesh: sa: 4 (over y, x), sb: 2 (over core), sc: 4 (over z).
Axes of the slice: x: 2, y: 2, z: 4, core: 2. Of those that a mesh axis runs over, the one named last changes fastest.
Arguments:
- queries: float32 [16384, 2048], P(('sa', 'sb', 'sc')), may hold values from -6 to 6
- key_rows: float32 [16384, 2048], P(('sa', 'sb', 'sc')), may hold values from -6 to 6
- value_rows: float32 [16384, 2048], P(('sa', 'sb', 'sc')), may hold values from -6 to 6
- out_grad: float32 [16384, 2048], P(('sa', 'sb', 'sc')), may hold values from -6 to 6
- prefix_state: float32 [16, 128, 128], replicated, may hold values from -768 to 768
- suffix_state: float32 [16, 128, 128], replicated, may hold values from -768 to 768
Outputs:
- query_grad: bfloat16 [16384, 2048], P(('sa', 'sb', 'sc'))
- key_grad: bfloat16 [16384, 2048], P(('sa', 'sb', 'sc'))
- value_grad: bfloat16 [16384, 2048], P(('sa', 'sb', 'sc'))
All inputs are finite; a program needn't handle non-finite values.
Results may differ from a plain program's by a relative error of at most 0.0019.
Values sent between devices are 32-bit elements; how exact they have to be, the bound alone decides.
No kernel may reach another device: no remote copies, remote signals or barrier semaphores. Data moves between devices by JAX's collectives and lax.ppermute only.
A program may use at most 576 MiB of HBM per device.

v0:
```python
import math

import jax
import jax.numpy as jnp
from jax import lax
from jax.sharding import PartitionSpec as P


def entering(part, axis, combine, identity):
    place = lax.axis_index(axis)
    gathered = jax.tree.map(lambda a: lax.all_gather(a, axis), part)
    state = jax.tree.map(lambda a, e: jnp.zeros_like(a) + jnp.asarray(e, a.dtype), part, identity)

    def one(hop, state):
        return combine(
            state, jax.tree.map(lambda a: lax.dynamic_index_in_dim(a, hop, 0, False), gathered)
        )

    return lax.fori_loop(0, place, one, state)


def add_states(earlier, later):
    return jax.tree.map(lambda left, right: left + right, earlier, later)


def run_chain(local_terms):
    zero_state = jax.tree.map(jnp.zeros_like, local_terms)
    inner_part = entering(local_terms, "sc", add_states, zero_state)
    group_sum = lax.psum((local_terms[0], local_terms[1]), "sc")
    middle_part = entering(group_sum, "sb", add_states, zero_state)
    block_sum = lax.psum((group_sum[0], group_sum[1]), "sb")
    outer_part = entering(block_sum, "sa", add_states, zero_state)
    return add_states(add_states(outer_part, middle_part), inner_part)


def shards(queries, key_rows, value_rows, out_grad, prefix_state, suffix_state):
    row_count = queries.shape[0]
    head_count = prefix_state.shape[0]
    head_size = prefix_state.shape[1]
    device_count = lax.axis_size("sa") * lax.axis_size("sb") * lax.axis_size("sc")
    factor = 1.0 / math.sqrt(head_size * row_count * device_count)
    highest = lax.Precision.HIGHEST
    shaped = (row_count, head_count, head_size)
    query_t = queries.reshape(shaped)
    key_t = key_rows.reshape(shaped)
    value_t = value_rows.reshape(shaped)
    grad_t = out_grad.reshape(shaped)
    kv_local = jnp.einsum("thd,the->hde", key_t, value_t, precision=highest)
    grad_local = jnp.einsum("the,thd->hed", grad_t, query_t, precision=highest)
    prior_kv, prior_grad = run_chain((kv_local, grad_local))
    total_grad = lax.psum(grad_local, ("sa", "sb", "sc"))
    state_before = prefix_state + prior_kv
    state_after = suffix_state + (total_grad - prior_grad - grad_local)
    lower = (
        lax.broadcasted_iota(jnp.int32, (row_count, row_count), 0)
        >= lax.broadcasted_iota(jnp.int32, (row_count, row_count), 1)
    ).astype(jnp.float32)
    grad_scores = jnp.einsum("the,she->hts", grad_t, value_t, precision=highest) * lower
    attn_scores = jnp.einsum("thd,shd->hts", query_t, key_t, precision=highest) * lower
    query_grad = factor * (
        jnp.einsum("the,hde->thd", grad_t, state_before, precision=highest)
        + jnp.einsum("hts,shd->thd", grad_scores, key_t, precision=highest)
    )
    key_grad = factor * (
        jnp.einsum("she,hed->shd", value_t, state_after, precision=highest)
        + jnp.einsum("hts,thd->shd", grad_scores, query_t, precision=highest)
    )
    value_grad = factor * (
        jnp.einsum("shd,hed->she", key_t, state_after, precision=highest)
        + jnp.einsum("hts,the->she", attn_scores, grad_t, precision=highest)
    )
    flat = (row_count, head_count * head_size)
    return (
        query_grad.astype(jnp.bfloat16).reshape(flat),
        key_grad.astype(jnp.bfloat16).reshape(flat),
        value_grad.astype(jnp.bfloat16).reshape(flat),
    )


def solution(mesh):
    return jax.shard_map(
        shards,
        mesh=mesh,
        in_specs=(
            P(("sa", "sb", "sc"), None),
            P(("sa", "sb", "sc"), None),
            P(("sa", "sb", "sc"), None),
            P(("sa", "sb", "sc"), None),
            P(),
            P(),
        ),
        out_specs=(
            P(("sa", "sb", "sc"), None),
            P(("sa", "sb", "sc"), None),
            P(("sa", "sb", "sc"), None),
        ),
        check_vma=False,
    )
```

profile of v0, /device:TPU:0, one launch (start us, length us, event | category | flops | bytes accessed | tf_op | source)
XLA Modules:
  0.0 535.8 jit_solution(6297481264336002140)
XLA Ops:
  8.0 11.2 %fusion.21 = f32[16,128,128]{2,1,0:T(8,128)} fusion(f32[512,2048]{1,0:T(8,128)} %param.14, f32[512,2048]{1,0:T(8,128)} %param.13), kind=kOutput, calls=%fused_computation.27 | convolution fusion | flops 1610612736 | bytes 9437184 | tf_op jit(solution)/shard_map/thd,the->hde/dot_general | solution.py:48
  19.2 5.1 copy.46
  24.3 5.9 %copy.27 = f32[512,16,128]{0,2,1:T(8,128)} copy(f32[512,16,128]{2,1,0:T(8,128)} %bitcast.130) | data formatting | bytes 8388608 | tf_op jit(solution)/shard_map/reshape | solution.py:47
  30.2 9.0 %fusion.16 = f32[16,128,128]{2,1,0:T(8,128)} fusion(f32[512,16,128]{0,2,1:T(8,128)} %copy.27, f32[512,2048]{1,0:T(8,128)} %param.12), kind=kOutput, calls=%fused_computation.22 | convolution fusion | flops 1610612736 | bytes 9437184 | tf_op jit(solution)/shard_map/the,thd->hed/dot_general | solution.py:49
  39.2 63.7 %all-gather.19.cloned.1.call-done = f32[64,128,128]{2,1,0:T(8,128)} async-done(((f32[16,128,128]{2,1,0:T(8,128)}), f32[64,128,128]{2,1,0:T(8,128)}) %all-gather.19.cloned.1.call-update) | async-done | bytes 4194320 | tf_op jit(solution)/shard_map/all_gather | solution.py:11
  103.6 88.6 %all-reduce.8.cloned.1.call-done = (f32[16,128,128]{2,1,0:T(8,128)}, f32[16,128,128]{2,1,0:T(8,128)}) async-done(((f32[16,128,128]{2,1,0:T(8,128)}, f32[16,128,128]{2,1,0:T(8,128)}), (f32[16,128,128]{2,1,0:T(8,128)}, f32[16,128,128]{2,1,0:T(8,128)})) %all-reduce.8.cloned.1.call-update) | async-done | bytes 2097168 | tf_op jit(solution)/shard_map/psum | solution.py:29
  192.9 10.6 %all-gather.15.cloned.1.call-done = f32[32,128,128]{2,1,0:T(8,128)} async-done(((f32[16,128,128]{2,1,0:T(8,128)}), f32[32,128,128]{2,1,0:T(8,128)}) %all-gather.15.cloned.1.call-update) | async-done | bytes 2097168 | tf_op jit(solution)/shard_map/all_gather | solution.py:11
  203.5 13.3 %all-gather.17.cloned.1.call-done = f32[32,128,128]{2,1,0:T(8,128)} async-done(((f32[16,128,128]{2,1,0:T(8,128)}), f32[32,128,128]{2,1,0:T(8,128)}) %all-gather.17.cloned.1.call-update) | async-done | bytes 2097168 | tf_op jit(solution)/shard_map/all_gather | solution.py:11
  217.9 24.3 %all-reduce.10.cloned.1.call-done = (f32[1,16,128,128]{3,2,1,0:T(8,128)}, f32[1,16,128,128]{3,2,1,0:T(8,128)}) async-done(((f32[1,16,128,128]{3,2,1,0:T(8,128)}, f32[1,16,128,128]{3,2,1,0:T(8,128)}), (f32[1,16,128,128]{3,2,1,0:T(8,128)}, f32[1,16,128,128]{3,2,1,0:T(8,128)})) %all-reduce.10.cloned.1.call-update) | async-done | bytes 2097168 | tf_op jit(solution)/shard_map/psum | solution.py:31
  243.8 19.5 %fusion.14 = f32[16,512,512]{2,1,0:T(8,128)} fusion(f32[512,2048]{1,0:T(8,128)} %param.12, f32[512,2048]{1,0:T(8,128)} %param.13), kind=kOutput, calls=%fused_computation.20 | convolution fusion | flops 6442450944 | bytes 25165824 | tf_op jit(solution)/shard_map/thd,shd->hts/dot_general | solution.py:59
  263.3 14.5 %fusion.11 = f32[16,512,512]{2,1,0:T(8,128)S(1)} fusion(f32[512,2048]{1,0:T(8,128)S(1)} %copy-done.4, f32[512,2048]{1,0:T(8,128)S(1)} %copy-done.5), kind=kOutput, calls=%fused_computation.17 | convolution fusion | flops 6442450944 | bytes 25165824 | tf_op jit(solution)/shard_map/the,she->hts/dot_general | solution.py:58
  277.8 14.5 %fusion.2 = f32[16,512,128]{1,2,0:T(8,128)} fusion(f32[16,512,512]{2,1,0:T(8,128)S(1)} %fusion.11, f32[512,512]{1,0:T(8,128)S(1)} %fusion.55, f32[512,2048]{1,0:T(8,128)} %param.12), kind=kOutput, calls=%fused_computation.8 | convolution fusion | flops 6446645248 | bytes 26214400 | tf_op jit(solution)/shard_map/hts,thd->shd/dot_general | solution.py:66
  292.3 21.3 %fusion.4 = f32[16,512,128]{1,2,0:T(8,128)} fusion(f32[16,512,512]{2,1,0:T(8,128)S(1)} %fusion.11, f32[512,512]{1,0:T(8,128)S(1)} %fusion.55, f32[512,2048]{1,0:T(8,128)} %param.13), kind=kOutput, calls=%fused_computation.10 | convolution fusion | flops 6446645248 | bytes 26214400 | tf_op jit(solution)/shard_map/hts,shd->thd/dot_general | solution.py:62
  313.6 14.2 %all-gather.21.cloned.1.call-done = f32[64,128,128]{2,1,0:T(8,128)} async-done(((f32[16,128,128]{2,1,0:T(8,128)}), f32[64,128,128]{2,1,0:T(8,128)}) %all-gather.21.cloned.1.call-update) | async-done | bytes 4194320 | tf_op jit(solution)/shard_map/all_gather | solution.py:11
  329.3 52.3 %all-gather.11.cloned.1.call-done = f32[4,16,128,128]{3,2,1,0:T(8,128)} async-done(((f32[1,16,128,128]{3,2,1,0:T(8,128)}), f32[4,16,128,128]{3,2,1,0:T(8,128)}) %all-gather.11.cloned.1.call-update) | async-done | bytes 4194320 | tf_op jit(solution)/shard_map/all_gather | solution.py:11
  381.5 55.0 %all-gather.13.cloned.1.call-done = f32[4,16,128,128]{3,2,1,0:T(8,128)} async-done(((f32[1,16,128,128]{3,2,1,0:T(8,128)}), f32[4,16,128,128]{3,2,1,0:T(8,128)}) %all-gather.13.cloned.1.call-update) | async-done | bytes 4194320 | tf_op jit(solution)/shard_map/all_gather | solution.py:11
  437.7 37.2 %all-reduce.6.cloned.1.call-done = f32[16,128,128]{2,1,0:T(8,128)} async-done(((f32[16,128,128]{2,1,0:T(8,128)}), f32[16,128,128]{2,1,0:T(8,128)}) %all-reduce.6.cloned.1.call-update) | async-done | bytes 1048592 | tf_op jit(solution)/shard_map/psum | solution.py:51
  479.4 3.8 fusion.23
  483.2 14.6 %fusion.29 = bf16[512,16,128]{0,2,1:T(8,128)(2,1)} fusion(f32[16,128,512]{2,1,0:T(8,128)S(1)} %fusion.23, f32[512,16,128]{0,2,1:T(8,128)S(1)} %copy-done.3, f32[16,512,512]{2,1,0:T(8,128)} %fusion.14, f32[512,512]{1,0:T(8,128)S(1)} %copy-done.7), kind=kOutput, calls=%fused_computation.36 | convolution fusion | flops 6449790976 | bytes 28311552 | tf_op jit(solution)/shard_map/hts,the->she/dot_general | solution.py:70
  497.8 3.9 copy.40
  501.7 9.2 %fusion.31 = bf16[512,16,128]{0,2,1:T(8,128)(2,1)} fusion(f32[16,512,128]{1,2,0:T(8,128)} %fusion.2, f32[16,128,128]{2,1,0:T(8,128)} %copy-done.8, f32[512,2048]{1,0:T(8,128)} %param.14), kind=kOutput, calls=%fused_computation.39 | convolution fusion | flops 1613758464 | bytes 11534336 | tf_op jit(solution)/shard_map/she,hed->shd/dot_general | solution.py:65
  510.9 4.1 copy.39
  515.0 9.2 %fusion.33 = bf16[512,16,128]{0,2,1:T(8,128)(2,1)} fusion(f32[16,512,128]{1,2,0:T(8,128)} %fusion.4, f32[16,128,128]{2,1,0:T(8,128)} %param.16, f32[16,128,128]{2,1,0:T(8,128)S(1)} %get-tuple-element.107, f32[16,128,128]{2,1,0:T(8,128)S(1)} %get-tuple-element.105, f32[16,128,128]{2,1,0:T(8,128)S(1)} %get-tuple-element.106, f32[512,2048]{1,0:T(8,128)} %param.15), kind=kOutput, calls=%fused_computation.42 | convolution fusion | flops 1614544896 | bytes 14680064 | tf_op jit(solution)/shard_map/the,hde->thd/dot_general | solution.py:61
  524.2 3.9 copy.38
  (47 shorter events, 11.0 us)
Async XLA Ops:
  8.0 94.9 %all-gather.19.cloned.1.call-start = ((), (), s32[]{:S(2)}) async-start(), calls=%async_computation.5 | async-start | bytes 5242880 | tf_op jit(solution)/shard_map/all_gather | solution.py:11
  102.9 89.4 %all-reduce.8.cloned.1.call-start = ((), (), s32[]{:S(2)}) async-start(), calls=%async_computation.7 | async-start | bytes 4194304 | tf_op jit(solution)/shard_map/psum | solution.py:29
  103.6 99.9 %all-gather.15.cloned.1.call-start = ((), (), s32[]{:S(2)}) async-start(), calls=%async_computation.3 | async-start | bytes 3145728 | tf_op jit(solution)/shard_map/all_gather | solution.py:11
  192.3 24.4 %all-gather.17.cloned.1.call-start = ((), (), s32[]{:S(2)}) async-start(), calls=%async_computation.4 | async-start | bytes 3145728 | tf_op jit(solution)/shard_map/all_gather | solution.py:11
  216.7 25.5 %all-reduce.10.cloned.1.call-start = ((), (), s32[]{:S(2)}) async-start(), calls=%async_computation.8 | async-start | bytes 4194304 | tf_op jit(solution)/shard_map/psum | solution.py:31
  217.3 110.5 %all-gather.21.cloned.1.call-start = ((), (), s32[]{:S(2)}) async-start(), calls=%async_computation.6 | async-start | bytes 5242880 | tf_op jit(solution)/shard_map/all_gather | solution.py:11
  217.9 163.6 %all-gather.11.cloned.1.call-start = ((), (), s32[]{:S(2)}) async-start(), calls=%async_computation | async-start | bytes 5242880 | tf_op jit(solution)/shard_map/all_gather | solution.py:11
  242.3 194.2 %all-gather.13.cloned.1.call-start = ((), (), s32[]{:S(2)}) async-start(), calls=%async_computation.1 | async-start | bytes 5242880 | tf_op jit(solution)/shard_map/all_gather | solution.py:11
  243.0 231.9 %all-reduce.6.cloned.1.call-start = ((), (), s32[]{:S(2)}) async-start(), calls=%async_computation.2 | async-start | bytes 2097152 | tf_op jit(solution)/shard_map/psum | solution.py:51
  243.7 48.6 %copy-start.6 = (f32[512,512]{1,0:T(8,128)}, f32[512,512]{1,0:T(8,128)S(1)}, u32[]{:S(2)}) copy-start(f32[512,512]{1,0:T(8,128)S(1)} %fusion.55) | copy-start | bytes 3145732
  243.7 19.6 %copy-start.4 = (f32[512,2048]{1,0:T(8,128)S(1)}, f32[512,2048]{1,0:T(8,128)}, u32[]{:S(2)}) copy-start(f32[512,2048]{1,0:T(8,128)} %param.15) | copy-start | bytes 12582916
  243.8 19.6 %copy-start.5 = (f32[512,2048]{1,0:T(8,128)S(1)}, f32[512,2048]{1,0:T(8,128)}, u32[]{:S(2)}) copy-start(f32[512,2048]{1,0:T(8,128)} %param.14) | copy-start | bytes 12582916
  328.1 1.0 copy-start.1
  329.3 52.3 %copy-start.2 = (f32[16,128,128]{2,1,0:T(8,128)}, f32[16,128,128]{2,1,0:T(8,128)S(1)}, u32[]{:S(2)}) copy-start(f32[16,128,128]{2,1,0:T(8,128)S(1)} %get-tuple-element.109) | copy-start | bytes 3145732
  474.9 4.5 copy-start
  478.4 1.0 copy-start.8
  479.4 3.8 copy-start.3
  479.4 3.8 copy-start.7
Sparse Core Ops, SparseCore 0:
  19.4 83.4 all-gather.18
  106.7 85.5 all-reduce.7
  193.9 9.5 all-gather.14
  205.0 11.7 all-gather.16
  219.8 22.4 all-reduce.9
  244.3 83.5 all-gather.20
  329.7 51.8 all-gather.10
  383.4 53.0 all-gather.12
Sparse Core Ops, SparseCore 1:
  249.3 225.6 all-reduce.5
where the time goes:
time: 542 us; the launch traced here: 536 us
  waiting for transfers between devices  363 us (67%)
  matrix products  127 us (23%)
  local copies, waits for them, and re-layouts  26.4 us (5%)
  between operations  16 us (3%)
    all_gather x6, waiting for transfers between devices, entering(): gathered = jax.tree.map(lambda a: lax.all_gather(a, axis), part)  209 us
    psum x1, waiting for transfers between devices, run_chain(): group_sum = lax.psum((local_terms[0], local_terms[1]), 'sc')  88.6 us
    psum x1, waiting for transfers between devices, shards(): total_grad = lax.psum(grad_local, ('sa', 'sb', 'sc'))  37.2 us
    psum x1, waiting for transfers between devices, run_chain(): block_sum = lax.psum((group_sum[0], group_sum[1]), 'sb')  24.3 us
    dot_general x1, matrix products, shards(): jnp.einsum('hts,shd->thd', grad_scores, key_t, precision=highest)  21.3 us
    dot_general x1, matrix products, shards(): jnp.einsum('thd,shd->hts', query_t, key_t, precision=highest) * lower  19.5 us
    unnamed x22, local copies, waits for them, and re-layouts  19 us
    dot_general x1, matrix products, shards(): jnp.einsum('hts,the->she', attn_scores, grad_t, precision=highest)  14.6 us
  transfers between devices with their start and end apart: 9, of which 9 were waited for; matrix products, arithmetic and copies ran while one was open for 17% of the time, Pallas kernels for 0%

commit v1 on v0

v1 whole, which is shorter than its diff:
```python
import functools
import math

import jax
import jax.numpy as jnp
from jax import lax
from jax.experimental import pallas as pl
from jax.experimental.pallas import tpu as pltpu
from jax.sharding import PartitionSpec as P

AXES = ("sa", "sb", "sc")
CUTS = ((4, False), (8, False), (4, True))
VMEM = 56 * 2**20
NN = (((1,), (0,)), ((), ()))
TN = (((0,), (0,)), ((), ()))


def split(x):
    high = x.astype(jnp.bfloat16)
    low = (x - high.astype(jnp.float32)).astype(jnp.bfloat16)
    return high, low


def wide(x):
    return jnp.concatenate(split(x), axis=1)


def fold(x):
    half = x.shape[1] // 2
    return x[:, :half] + x[:, half:]


def stacked(x):
    return jnp.concatenate([x, x], axis=0)


def dot(a, b):
    return lax.dot_general(a, b, NN, preferred_element_type=jnp.float32)


def outer(a, b):
    half = a.shape[1]
    full = fold(lax.dot_general(wide(a), wide(b), TN, preferred_element_type=jnp.float32))
    return full[:half] + full[half:]


def local_kernel(place_ref, q_ref, k_ref, v_ref, g_ref, out_ref):
    size = out_ref.shape[-1]
    for j in range(out_ref.shape[1]):
        columns = slice(j * size, (j + 1) * size)
        out_ref[0, j] = outer(k_ref[:, columns], v_ref[:, columns])
        out_ref[1, j] = outer(g_ref[:, columns], q_ref[:, columns])


def local_terms(first, count, arrays, size):
    rows = arrays[0].shape[0]
    step = 2 - count % 2
    place = (first // step).reshape(1).astype(jnp.int32)
    spec = pl.BlockSpec((rows, step * size), lambda i, place: (0, place[0] + i))
    return pl.pallas_call(
        local_kernel,
        grid_spec=pltpu.PrefetchScalarGridSpec(
            num_scalar_prefetch=1,
            grid=(count // step,),
            in_specs=[spec] * 4,
            out_specs=pl.BlockSpec((2, step, size, size), lambda i, place: (0, i, 0, 0)),
        ),
        out_shape=jax.ShapeDtypeStruct((2, count, size, size), jnp.float32),
        compiler_params=pltpu.CompilerParams(vmem_limit_bytes=VMEM),
        cost_estimate=pl.CostEstimate(
            flops=16 * count * rows * size * size, bytes_accessed=16 * count * rows * size, transcendentals=0
        ),
        name="local_terms",
    )(place, *arrays)


def head_grads(q, k, v, g, before, after):
    count, size = len(q), q[0].shape[1]
    row = lax.broadcasted_iota(jnp.int32, (size, size), 0)
    column = lax.broadcasted_iota(jnp.int32, (size, size), 1)
    lower, upper = row >= column, row <= column

    q_t, v_t, g_t = ([wide(x.T) for x in xs] for xs in (q, v, g))
    q, k, v, g = ([wide(x) for x in xs] for xs in (q, k, v, g))
    q_rows, k_rows, g_rows = ([stacked(x) for x in xs] for xs in (q, k, g))

    before_t, after, after_t = [before.T], [after], [after.T]
    for i in range(count - 1):
        j = count - 1 - i
        before_t.append(before_t[-1] + fold(dot(v_t[i], k_rows[i])))
        after.append(after[-1] + fold(dot(g_t[j], q_rows[j])))
        after_t.append(after[-1].T)
    after, after_t = after[::-1], after_t[::-1]

    def scores(a, b_t, mask):
        return wide(jnp.where(mask, fold(dot(a, stacked(b_t))), 0.0))

    def both(rows, state, weights, other_rows):
        left = jnp.concatenate([rows, weights], axis=1)
        right = jnp.concatenate([stacked(wide(state)), other_rows], axis=0)
        return fold(dot(left, right))

    for i in range(count):
        yield (
            both(g[i], before_t[i], scores(g[i], v_t[i], lower), k_rows[i]),
            both(v[i], after[i], scores(v[i], g_t[i], upper), q_rows[i]),
            both(k[i], after_t[i], scores(k[i], q_t[i], upper), g_rows[i]),
        )


def grads_kernel(factor, place_ref, q_ref, k_ref, v_ref, g_ref, state_ref, *rest):
    outs = rest[-3:]
    size = state_ref.shape[-1]
    for j in range(state_ref.shape[1]):
        columns = slice(j * size, (j + 1) * size)
        blocks = [
            [ref[i : i + size, columns] for i in range(0, q_ref.shape[0], size)]
            for ref in (q_ref, k_ref, v_ref, g_ref)
        ]
        for i, results in enumerate(head_grads(*blocks, state_ref[0, j], state_ref[1, j])):
            for ref, x in zip(outs, results):
                ref[i * size : (i + 1) * size, columns] = (factor * x).astype(ref.dtype)


def grads(first, arrays, state, outs, factor):
    rows, columns = arrays[0].shape
    count, size = state.shape[1], state.shape[2]
    step = 2 - count % 2
    place = (first // step).reshape(1).astype(jnp.int32)
    spec = pl.BlockSpec((rows, step * size), lambda i, place: (0, place[0] + i))
    state_spec = pl.BlockSpec((2, step, size, size), lambda i, place: (0, i, 0, 0))
    given = [] if outs is None else list(outs)
    return pl.pallas_call(
        functools.partial(grads_kernel, factor),
        grid_spec=pltpu.PrefetchScalarGridSpec(
            num_scalar_prefetch=1,
            grid=(count // step,),
            in_specs=[spec] * 4 + [state_spec] + [pl.BlockSpec(memory_space=pl.ANY)] * len(given),
            out_specs=[spec] * 3,
        ),
        out_shape=[jax.ShapeDtypeStruct((rows, columns), jnp.bfloat16)] * 3,
        input_output_aliases={6 + i: i for i in range(len(given))},
        compiler_params=pltpu.CompilerParams(vmem_limit_bytes=VMEM),
        cost_estimate=pl.CostEstimate(
            flops=96 * count * rows * size * size, bytes_accessed=22 * count * rows * size, transcendentals=0
        ),
        name="grads",
    )(place, *arrays, state, *given)


def swap(x, axis, offset):
    return lax.ppermute(x, axis, [(i, i ^ offset) for i in range(lax.axis_size(axis))])


def plane_sums(total):
    a, b = lax.axis_index("sa"), lax.axis_index("sb")
    kv = grad = jnp.zeros_like(total[0])
    chip = total
    for k in range(1, lax.axis_size("sb")):
        other = swap(total, "sb", k)
        chip = chip + other
        low = (b ^ k) < b
        kv = kv + jnp.where(low, other[0], 0.0)
        grad = grad + jnp.where(low, 0.0, other[1])
    for k in range(1, lax.axis_size("sa")):
        low = (a ^ k) < a
        other = swap(jnp.where(low, chip[1], chip[0]), "sa", k)
        kv = kv + jnp.where(low, other, 0.0)
        grad = grad + jnp.where(low, 0.0, other)
    return jnp.stack([kv, grad])


def shards(queries, key_rows, value_rows, out_grad, prefix_state, suffix_state):
    rows = queries.shape[0]
    head_count, size = prefix_state.shape[0], prefix_state.shape[1]
    devices = lax.axis_size("sa") * lax.axis_size("sb") * lax.axis_size("sc")
    factor = 1.0 / math.sqrt(size * rows * devices)
    c = lax.axis_index("sc")
    odd = c % 2
    arrays = (queries, key_rows, value_rows, out_grad)

    chunks, start = [], 0
    for heads, plane_first in CUTS:
        half = heads // 2
        own = start + odd * half
        his = start + (1 - odd) * half
        edge = jnp.stack(
            [lax.dynamic_slice_in_dim(s, own, half, 0) for s in (prefix_state, suffix_state)]
        )
        chunks.append((own, his, edge, plane_first))
        start += heads

    local = []
    for own, his, edge, plane_first in chunks:
        mine_his = local_terms(his, edge.shape[1], arrays, size)
        his_own = swap(mine_his, "sc", 1)
        mine_own = local_terms(own, edge.shape[1], arrays, size)
        local.append((mine_own, his_own))

    states = []
    for (own, his, edge, plane_first), (mine_own, his_own) in zip(chunks, local):
        pair = mine_own + his_own
        if plane_first:
            plane = plane_sums(pair)
            state = edge + plane
            for k in range(2, lax.axis_size("sc"), 2):
                low = (c ^ k) < c
                sent = plane + jnp.stack([jnp.where(low, 0.0, pair[0]), jnp.where(low, pair[1], 0.0)])
                state = state + swap(sent, "sc", k)
        else:
            total, state = pair, edge
            for k in range(2, lax.axis_size("sc"), 2):
                other = swap(pair, "sc", k)
                total = total + other
                low = (c ^ k) < c
                state = state + jnp.stack([jnp.where(low, other[0], 0.0), jnp.where(low, 0.0, other[1])])
            state = state + plane_sums(total)
        upper = odd == 1
        state_own = state + jnp.stack([jnp.where(upper, his_own[0], 0.0), jnp.where(upper, 0.0, his_own[1])])
        state_his = state + jnp.stack([jnp.where(upper, 0.0, mine_own[0]), jnp.where(upper, mine_own[1], 0.0)])
        states.append((state_own, swap(state_his, "sc", 1)))

    outs = None
    for (own, his, edge, plane_first), (state_own, state_other) in zip(chunks, states):
        outs = grads(own, arrays, state_own, outs, factor)
        outs = grads(his, arrays, state_other, outs, factor)
    return tuple(outs)


def solution(mesh):
    rows = P(AXES, None)
    return jax.shard_map(
        shards,
        mesh=mesh,
        in_specs=(rows, rows, rows, rows, P(), P()),
        out_specs=(rows, rows, rows),
        check_vma=False,
    )
```

time: 542 us -> 126 us (0.23); the launches traced: 536 us -> 126 us
  waiting for transfers between devices: 363 us -> 42.5 us
  matrix products: 127 us -> 0 us
  Pallas kernels: 0 us -> 52.6 us
  local copies, waits for them, and re-layouts: 26.4 us -> 2.29 us
  starting transfers between devices: 0.27 us -> 21.7 us
  between operations: 16 us -> 0.99 us
    all_gather x6 -> x0, waiting for transfers between devices: 209 us -> none  [entering(): gathered = jax.tree.map(lambda a: lax.all_gather(a, axis), part)]
    psum x3 -> x0, waiting for transfers between devices: 150 us -> none  [the longest x1 88.6 us: run_chain(): group_sum = lax.psum((local_terms[0], local_terms[1]), 'sc')]
    dot_general x10 -> x0, matrix products: 127 us -> none  [the longest x1 21.3 us: shards(): jnp.einsum('hts,shd->thd', grad_scores, key_t, precision=highest)]
    pallas_call x0 -> x12, Pallas kernels: none -> 52.6 us  [the longest x6 34.7 us: grads(): pl.pallas_call(functools.partial(grads_kernel, factor), grid_spec=pltpu.P...]
    ppermute x0 -> x21, waiting for transfers between devices: none -> 42.5 us  [swap(): lax.ppermute(x, axis, [(i, i ^ offset) for i in range(lax.axis_size(axis))])]
    ppermute x0 -> x21, starting transfers between devices: none -> 21.7 us  [swap(): lax.ppermute(x, axis, [(i, i ^ offset) for i in range(lax.axis_size(axis))])]
    unnamed x22 -> x16, local copies, waits for them, and re-layouts: 19 us -> 2.21 us
    reshape x1 -> x0, local copies, waits for them, and re-layouts: 5.88 us -> none  [shards(): grad_t = out_grad.reshape(shaped)]
  transfers between devices with their start and end apart: 9 -> 21, of which waited for: 9 -> 7; matrix products, arithmetic and copies ran while one was open for 17% -> 4% of each run, Pallas kernels for 0% -> 36%
where the time goes in v1:
time: 126 us
  Pallas kernels  52.6 us (42%)
  waiting for transfers between devices  42.5 us (34%)
  starting transfers between devices  21.7 us (17%)
  other arithmetic  5.47 us (4%)
  local copies, waits for them, and re-layouts  2.29 us (2%)
    ppermute x21, waiting for transfers between devices, swap(): lax.ppermute(x, axis, [(i, i ^ offset) for i in range(lax.axis_size(axis))])  42.5 us
    pallas_call x6, Pallas kernels, grads(): pl.pallas_call(functools.partial(grads_kernel, factor), grid_spec=pltpu.P...  34.7 us
    ppermute x21, starting transfers between devices, swap(): lax.ppermute(x, axis, [(i, i ^ offset) for i in range(lax.axis_size(axis))])  21.7 us
    pallas_call x6, Pallas kernels, local_terms(): pl.pallas_call(local_kernel, grid_spec=pltpu.PrefetchScalarGridSpec(num_s...  17.9 us
  transfers between devices with their start and end apart: 21, of which 7 were waited for; matrix products, arithmetic and copies ran while one was open for 4% of the time, Pallas kernels for 36%

profile of v1, /device:TPU:0, one launch (start us, length us, event | category | flops | bytes accessed | tf_op | source)
XLA Modules:
  0.0 125.6 jit_solution(1804622196606370433)
XLA Ops:
  0.7 2.7 %local_terms.11 = f32[2,2,128,128]{3,2,1,0:T(8,128)} custom-call(s32[1]{0:T(128)} %bitcast.22.place_ref, f32[512,2048]{1,0:T(8,128)} %q_ref.23, f32[512,2048]{1,0:T(8,128)} %k_ref.23, f32[512,2048]{1,0:T(8,128)} %v_ref.23, f32[512,2048]{1,0:T(8,128)} %g_ref.23), custom_call_target="tpu_custom_call" | custom-call | flops 268435456 | bytes 2097152 | tf_op jit(solution)/shard_map/local_terms/pallas_call | solution.py:60
  3.4 3.0 %collective-permute-start.14 = (f32[2,2,128,128]{3,2,1,0:T(8,128)}, f32[2,2,128,128]{3,2,1,0:T(8,128)S(1)}, u32[]{:S(2)}, u32[]{:S(2)}) collective-permute-start(f32[2,2,128,128]{3,2,1,0:T(8,128)} %local_terms.11), channel_id=1, source_target_pairs={{0,1},{1,0},{2,3},{3,2},{4,5},{5,4},{6,7},{7,6},{8,9},{9,8},{10,11... | collective-permute-start | bytes 786440 | tf_op jit(solution)/shard_map/ppermute | solution.py:152
  6.4 3.4 %local_terms.9 = f32[2,4,128,128]{3,2,1,0:T(8,128)} custom-call(s32[1]{0:T(128)} %bitcast.11.place_ref, f32[512,2048]{1,0:T(8,128)} %q_ref.23, f32[512,2048]{1,0:T(8,128)} %k_ref.23, f32[512,2048]{1,0:T(8,128)} %v_ref.23, f32[512,2048]{1,0:T(8,128)} %g_ref.23), custom_call_target="tpu_custom_call" | custom-call | flops 536870912 | bytes 4194304 | tf_op jit(solution)/shard_map/local_terms/pallas_call | solution.py:60
  9.8 2.7 %local_terms.7 = f32[2,2,128,128]{3,2,1,0:T(8,128)} custom-call(s32[1]{0:T(128)} %bitcast.place_ref, f32[512,2048]{1,0:T(8,128)} %q_ref.23, f32[512,2048]{1,0:T(8,128)} %k_ref.23, f32[512,2048]{1,0:T(8,128)} %v_ref.23, f32[512,2048]{1,0:T(8,128)} %g_ref.23), custom_call_target="tpu_custom_call" | custom-call | flops 268435456 | bytes 2097152 | tf_op jit(solution)/shard_map/local_terms/pallas_call | solution.py:60
  12.6 2.0 %collective-permute-start = (f32[2,2,128,128]{3,2,1,0:T(8,128)}, f32[2,2,128,128]{3,2,1,0:T(8,128)S(1)}, u32[]{:S(2)}, u32[]{:S(2)}) collective-permute-start(f32[2,2,128,128]{3,2,1,0:T(8,128)} %local_terms.7), channel_id=1, source_target_pairs={{0,1},{1,0},{2,3},{3,2},{4,5},{5,4},{6,7},{7,6},{8,9},{9,8},{10,11... | collective-permute-start | bytes 786440 | tf_op jit(solution)/shard_map/ppermute | solution.py:152
  14.6 2.7 %local_terms.10 = f32[2,2,128,128]{3,2,1,0:T(8,128)} custom-call(s32[1]{0:T(128)} %bitcast.25.place_ref, f32[512,2048]{1,0:T(8,128)} %q_ref.23, f32[512,2048]{1,0:T(8,128)} %k_ref.23, f32[512,2048]{1,0:T(8,128)} %v_ref.23, f32[512,2048]{1,0:T(8,128)} %g_ref.23), custom_call_target="tpu_custom_call" | custom-call | flops 268435456 | bytes 2097152 | tf_op jit(solution)/shard_map/local_terms/pallas_call | solution.py:60
  17.3 2.9 %local_terms.6 = f32[2,2,128,128]{3,2,1,0:T(8,128)} custom-call(s32[1]{0:T(128)} %bitcast.3.place_ref, f32[512,2048]{1,0:T(8,128)} %q_ref.23, f32[512,2048]{1,0:T(8,128)} %k_ref.23, f32[512,2048]{1,0:T(8,128)} %v_ref.23, f32[512,2048]{1,0:T(8,128)} %g_ref.23), custom_call_target="tpu_custom_call" | custom-call | flops 268435456 | bytes 2097152 | tf_op jit(solution)/shard_map/local_terms/pallas_call | solution.py:60
  21.3 3.4 %local_terms.8 = f32[2,4,128,128]{3,2,1,0:T(8,128)} custom-call(s32[1]{0:T(128)} %bitcast.14.place_ref, f32[512,2048]{1,0:T(8,128)} %q_ref.23, f32[512,2048]{1,0:T(8,128)} %k_ref.23, f32[512,2048]{1,0:T(8,128)} %v_ref.23, f32[512,2048]{1,0:T(8,128)} %g_ref.23), custom_call_target="tpu_custom_call" | custom-call | flops 536870912 | bytes 4194304 | tf_op jit(solution)/shard_map/local_terms/pallas_call | solution.py:60
  25.9 2.7 %collective-permute-start.15 = (f32[2,2,128,128]{3,2,1,0:T(8,128)S(1)}, f32[2,2,128,128]{3,2,1,0:T(8,128)S(1)}, u32[]{:S(2)}, u32[]{:S(2)}) collective-permute-start(f32[2,2,128,128]{3,2,1,0:T(8,128)S(1)} %add.189), channel_id=1, source_target_pairs={{0,2},{1,3},{2,0},{3,1},{4,6},{5,7},{6,4},{7,5},{8,10},{9,11},{10,... | collective-permute-start | bytes 786440 | tf_op jit(solution)/shard_map/ppermute | solution.py:152
  28.5 4.8 %collective-permute-done = f32[2,2,128,128]{3,2,1,0:T(8,128)S(1)} collective-permute-done((f32[2,2,128,128]{3,2,1,0:T(8,128)}, f32[2,2,128,128]{3,2,1,0:T(8,128)S(1)}, u32[]{:S(2)}, u32[]{:S(2)}) %collective-permute-start) | collective-permute-done | bytes 262176 | tf_op jit(solution)/shard_map/ppermute | solution.py:152
  33.6 6.2 %collective-permute-done.15 = f32[2,2,128,128]{3,2,1,0:T(8,128)S(1)} collective-permute-done((f32[2,2,128,128]{3,2,1,0:T(8,128)S(1)}, f32[2,2,128,128]{3,2,1,0:T(8,128)S(1)}, u32[]{:S(2)}, u32[]{:S(2)}) %collective-permute-start.15) | collective-permute-done | bytes 262176 | tf_op jit(solution)/shard_map/ppermute | solution.py:152
  40.1 1.5 %collective-permute-start.2 = (f32[2,128,128]{2,1,0:T(8,128)S(1)}, f32[2,128,128]{2,1,0:T(8,128)S(1)}, u32[]{:S(2)}, u32[]{:S(2)}) collective-permute-start(f32[2,128,128]{2,1,0:T(8,128)S(1)} %get-tuple-element.69), channel_id=1, source_target_pairs={{0,8},{8,0},{16,24},{24,16},{1,9},{9,1},{17,25},{25,17},{2,10},{10... | collective-permute-start | bytes 393224 | tf_op jit(solution)/shard_map/ppermute | solution.py:152
  43.8 1.5 %collective-permute-start.17 = (f32[2,128,128]{2,1,0:T(8,128)S(1)}, f32[2,128,128]{2,1,0:T(8,128)S(1)}, u32[]{:S(2)}, u32[]{:S(2)}) collective-permute-start(f32[2,128,128]{2,1,0:T(8,128)S(1)} %get-tuple-element.62), channel_id=1, source_target_pairs={{0,8},{8,0},{16,24},{24,16},{1,9},{9,1},{17,25},{25,17},{2,10},{10... | collective-permute-start | bytes 393224 | tf_op jit(solution)/shard_map/ppermute | solution.py:152
  45.4 20.9 %collective-permute-done.8 = f32[2,4,128,128]{3,2,1,0:T(8,128)S(1)} collective-permute-done((f32[2,4,128,128]{3,2,1,0:T(8,128)S(1)}, f32[2,4,128,128]{3,2,1,0:T(8,128)S(1)}, u32[]{:S(2)}, u32[]{:S(2)}) %collective-permute-start.8) | collective-permute-done | bytes 524320 | tf_op jit(solution)/shard_map/ppermute | solution.py:152
  69.6 5.0 %collective-permute-done.18 = f32[2,128,128]{2,1,0:T(8,128)S(1)} collective-permute-done((f32[2,128,128]{2,1,0:T(8,128)S(1)}, f32[2,128,128]{2,1,0:T(8,128)S(1)}, u32[]{:S(2)}, u32[]{:S(2)}) %collective-permute-start.18) | collective-permute-done | bytes 131104 | tf_op jit(solution)/shard_map/ppermute | solution.py:152
  75.5 1.6 %collective-permute-start.10 = (f32[4,128,128]{2,1,0:T(8,128)S(1)}, f32[4,128,128]{2,1,0:T(8,128)S(1)}, u32[]{:S(2)}, u32[]{:S(2)}) collective-permute-start(f32[4,128,128]{2,1,0:T(8,128)S(1)} %get-tuple-element.53), channel_id=1, source_target_pairs={{0,8},{8,0},{16,24},{24,16},{1,9},{9,1},{17,25},{25,17},{2,10},{10... | collective-permute-start | bytes 786440 | tf_op jit(solution)/shard_map/ppermute | solution.py:152
  79.1 4.9 %grads.6 = (bf16[512,2048]{1,0:T(8,128)(2,1)}, bf16[512,2048]{1,0:T(8,128)(2,1)}, bf16[512,2048]{1,0:T(8,128)(2,1)}) custom-call(s32[1]{0:T(128)} %bitcast.25.place_ref, f32[512,2048]{1,0:T(8,128)} %q_ref.23, f32[512,2048]{1,0:T(8,128)} %k_ref.23, f32[512,2048]{1,0:T(8,128)} %v_ref.23, f32[512,2048]{1,0:T(8,128)} %g_ref.23, ...), custom_call_target="tpu_custom_call" | custom-call | flops 1610612736 | bytes 2883584 | tf_op jit(solution)/shard_map/grads/pallas_call | solution.py:133
  84.8 4.1 %collective-permute-done.11 = f32[4,128,128]{2,1,0:T(8,128)S(1)} collective-permute-done((f32[4,128,128]{2,1,0:T(8,128)S(1)}, f32[4,128,128]{2,1,0:T(8,128)S(1)}, u32[]{:S(2)}, u32[]{:S(2)}) %collective-permute-start.11) | collective-permute-done | bytes 262176 | tf_op jit(solution)/shard_map/ppermute | solution.py:152
  91.5 2.0 %collective-permute-start.6 = (f32[2,2,128,128]{3,2,1,0:T(8,128)S(1)}, f32[2,2,128,128]{3,2,1,0:T(8,128)S(1)}, u32[]{:S(2)}, u32[]{:S(2)}) collective-permute-start(f32[2,2,128,128]{3,2,1,0:T(8,128)S(1)} %get-tuple-element.44), channel_id=1, source_target_pairs={{0,1},{1,0},{2,3},{3,2},{4,5},{5,4},{6,7},{7,6},{8,9},{9,8},{10,11... | collective-permute-start | bytes 786440 | tf_op jit(solution)/shard_map/ppermute | solution.py:152
  94.2 4.9 %grads.7 = (bf16[512,2048]{1,0:T(8,128)(2,1)}, bf16[512,2048]{1,0:T(8,128)(2,1)}, bf16[512,2048]{1,0:T(8,128)(2,1)}) custom-call(s32[1]{0:T(128)} %bitcast.22.place_ref, f32[512,2048]{1,0:T(8,128)} %q_ref.23, f32[512,2048]{1,0:T(8,128)} %k_ref.23, f32[512,2048]{1,0:T(8,128)} %v_ref.23, ...), custom_call_target="tpu_custom_call", output_to_operand_aliasing={{0}: (6, {}), {1}: (7, {}), {2}: (8, {})} | custom-call | flops 1610612736 | bytes 2883584 | tf_op jit(solution)/shard_map/grads/pallas_call | solution.py:133
  99.1 7.7 %grads.8 = (bf16[512,2048]{1,0:T(8,128)(2,1)}, bf16[512,2048]{1,0:T(8,128)(2,1)}, bf16[512,2048]{1,0:T(8,128)(2,1)}) custom-call(s32[1]{0:T(128)} %bitcast.14.place_ref, f32[512,2048]{1,0:T(8,128)} %q_ref.23, f32[512,2048]{1,0:T(8,128)} %k_ref.23, f32[512,2048]{1,0:T(8,128)} %v_ref.23, ...), custom_call_target="tpu_custom_call", output_to_operand_aliasing={{0}: (6, {}), {1}: (7, {}), {2}: (8, {})} | custom-call | flops 3221225472 | bytes 5767168 | tf_op jit(solution)/shard_map/grads/pallas_call | solution.py:133
  107.6 7.5 %grads.9 = (bf16[512,2048]{1,0:T(8,128)(2,1)}, bf16[512,2048]{1,0:T(8,128)(2,1)}, bf16[512,2048]{1,0:T(8,128)(2,1)}) custom-call(s32[1]{0:T(128)} %bitcast.11.place_ref, f32[512,2048]{1,0:T(8,128)} %q_ref.23, f32[512,2048]{1,0:T(8,128)} %k_ref.23, f32[512,2048]{1,0:T(8,128)} %v_ref.23, ...), custom_call_target="tpu_custom_call", output_to_operand_aliasing={{0}: (6, {}), {1}: (7, {}), {2}: (8, {})} | custom-call | flops 3221225472 | bytes 5767168 | tf_op jit(solution)/shard_map/grads/pallas_call | solution.py:133
  115.1 4.9 %grads.10 = (bf16[512,2048]{1,0:T(8,128)(2,1)}, bf16[512,2048]{1,0:T(8,128)(2,1)}, bf16[512,2048]{1,0:T(8,128)(2,1)}) custom-call(s32[1]{0:T(128)} %bitcast.3.place_ref, f32[512,2048]{1,0:T(8,128)} %q_ref.23, f32[512,2048]{1,0:T(8,128)} %k_ref.23, f32[512,2048]{1,0:T(8,128)} %v_ref.23, ...), custom_call_target="tpu_custom_call", output_to_operand_aliasing={{0}: (6, {}), {1}: (7, {}), {2}: (8, {})} | custom-call | flops 1610612736 | bytes 2883584 | tf_op jit(solution)/shard_map/grads/pallas_call | solution.py:133
  120.7 4.9 %grads.11 = (bf16[512,2048]{1,0:T(8,128)(2,1)}, bf16[512,2048]{1,0:T(8,128)(2,1)}, bf16[512,2048]{1,0:T(8,128)(2,1)}) custom-call(s32[1]{0:T(128)} %bitcast.place_ref, f32[512,2048]{1,0:T(8,128)} %q_ref.23, f32[512,2048]{1,0:T(8,128)} %k_ref.23, f32[512,2048]{1,0:T(8,128)} %v_ref.23, ...), custom_call_target="tpu_custom_call", output_to_operand_aliasing={{0}: (6, {}), {1}: (7, {}), {2}: (8, {})} | custom-call | flops 1610612736 | bytes 2883584 | tf_op jit(solution)/shard_map/grads/pallas_call | solution.py:133
  (75 shorter events, 16.7 us)
Async XLA Ops:
  3.4 22.4 %collective-permute-start.14 = (f32[2,2,128,128]{3,2,1,0:T(8,128)}, f32[2,2,128,128]{3,2,1,0:T(8,128)S(1)}, u32[]{:S(2)}, u32[]{:S(2)}) collective-permute-start(f32[2,2,128,128]{3,2,1,0:T(8,128)} %local_terms.11), channel_id=1, source_target_pairs={{0,1},{1,0},{2,3},{3,2},{4,5},{5,4},{6,7},{7,6},{8,9},{9,8},{10,11... | collective-permute-start | bytes 786440 | tf_op jit(solution)/shard_map/ppermute | solution.py:152
  9.8 30.1 %collective-permute-start.7 = (f32[2,4,128,128]{3,2,1,0:T(8,128)}, f32[2,4,128,128]{3,2,1,0:T(8,128)S(1)}, u32[]{:S(2)}, u32[]{:S(2)}) collective-permute-start(f32[2,4,128,128]{3,2,1,0:T(8,128)} %local_terms.9), channel_id=1, source_target_pairs={{0,1},{1,0},{2,3},{3,2},{4,5},{5,4},{6,7},{7,6},{8,9},{9,8},{10,11... | collective-permute-start | bytes 1572872 | tf_op jit(solution)/shard_map/ppermute | solution.py:152
  12.6 20.8 %collective-permute-start = (f32[2,2,128,128]{3,2,1,0:T(8,128)}, f32[2,2,128,128]{3,2,1,0:T(8,128)S(1)}, u32[]{:S(2)}, u32[]{:S(2)}) collective-permute-start(f32[2,2,128,128]{3,2,1,0:T(8,128)} %local_terms.7), channel_id=1, source_target_pairs={{0,1},{1,0},{2,3},{3,2},{4,5},{5,4},{6,7},{7,6},{8,9},{9,8},{10,11... | collective-permute-start | bytes 786440 | tf_op jit(solution)/shard_map/ppermute | solution.py:152
  17.3 3.9 %copy-start.7 = (f32[16,128,128]{2,1,0:T(8,128)S(1)}, f32[16,128,128]{2,1,0:T(8,128)}, u32[]{:S(2)}) copy-start(f32[16,128,128]{2,1,0:T(8,128)} %param.10) | copy-start | bytes 3145732
  21.3 12.1 %copy-start.2 = (f32[2,2,128,128]{3,2,1,0:T(8,128)S(1)}, f32[2,2,128,128]{3,2,1,0:T(8,128)}, u32[]{:S(2)}) copy-start(f32[2,2,128,128]{3,2,1,0:T(8,128)} %local_terms.6) | copy-start | bytes 786436
  25.8 14.0 %copy-start = (f32[2,4,128,128]{3,2,1,0:T(8,128)S(1)}, f32[2,4,128,128]{3,2,1,0:T(8,128)}, u32[]{:S(2)}) copy-start(f32[2,4,128,128]{3,2,1,0:T(8,128)} %local_terms.8) | copy-start | bytes 1572868
  25.9 13.8 %collective-permute-start.15 = (f32[2,2,128,128]{3,2,1,0:T(8,128)S(1)}, f32[2,2,128,128]{3,2,1,0:T(8,128)S(1)}, u32[]{:S(2)}, u32[]{:S(2)}) collective-permute-start(f32[2,2,128,128]{3,2,1,0:T(8,128)S(1)} %add.189), channel_id=1, source_target_pairs={{0,2},{1,3},{2,0},{3,1},{4,6},{5,7},{6,4},{7,5},{8,10},{9,11},{10,... | collective-permute-start | bytes 786440 | tf_op jit(solution)/shard_map/ppermute | solution.py:152
  33.4 6.6 %collective-permute-start.1 = (f32[2,2,128,128]{3,2,1,0:T(8,128)S(1)}, f32[2,2,128,128]{3,2,1,0:T(8,128)S(1)}, u32[]{:S(2)}, u32[]{:S(2)}) collective-permute-start(f32[2,2,128,128]{3,2,1,0:T(8,128)S(1)} %add.159), channel_id=1, source_target_pairs={{0,4},{4,0},{1,5},{5,1},{2,6},{6,2},{3,7},{7,3},{8,12},{12,8},{9,1... | collective-permute-start | bytes 786440 | tf_op jit(solution)/shard_map/ppermute | solution.py:152
  39.8 4.0 %collective-permute-start.16 = (f32[2,2,128,128]{3,2,1,0:T(8,128)S(1)}, f32[2,2,128,128]{3,2,1,0:T(8,128)S(1)}, u32[]{:S(2)}, u32[]{:S(2)}) collective-permute-start(f32[2,2,128,128]{3,2,1,0:T(8,128)S(1)} %add.191), channel_id=1, source_target_pairs={{0,4},{4,0},{1,5},{5,1},{2,6},{6,2},{3,7},{7,3},{8,12},{12,8},{9,1... | collective-permute-start | bytes 786440 | tf_op jit(solution)/shard_map/ppermute | solution.py:152
  39.9 26.3 %collective-permute-start.8 = (f32[2,4,128,128]{3,2,1,0:T(8,128)S(1)}, f32[2,4,128,128]{3,2,1,0:T(8,128)S(1)}, u32[]{:S(2)}, u32[]{:S(2)}) collective-permute-start(f32[2,4,128,128]{3,2,1,0:T(8,128)S(1)} %add.175), channel_id=1, source_target_pairs={{0,2},{1,3},{2,0},{3,1},{4,6},{5,7},{6,4},{7,5},{8,10},{9,11},{10,... | collective-permute-start | bytes 1572872 | tf_op jit(solution)/shard_map/ppermute | solution.py:152
  40.1 27.8 %collective-permute-start.2 = (f32[2,128,128]{2,1,0:T(8,128)S(1)}, f32[2,128,128]{2,1,0:T(8,128)S(1)}, u32[]{:S(2)}, u32[]{:S(2)}) collective-permute-start(f32[2,128,128]{2,1,0:T(8,128)S(1)} %get-tuple-element.69), channel_id=1, source_target_pairs={{0,8},{8,0},{16,24},{24,16},{1,9},{9,1},{17,25},{25,17},{2,10},{10... | collective-permute-start | bytes 393224 | tf_op jit(solution)/shard_map/ppermute | solution.py:152
  41.6 27.7 %collective-permute-start.3 = (f32[2,128,128]{2,1,0:T(8,128)S(1)}, f32[2,128,128]{2,1,0:T(8,128)S(1)}, u32[]{:S(2)}, u32[]{:S(2)}) collective-permute-start(f32[2,128,128]{2,1,0:T(8,128)S(1)} %get-tuple-element.71), channel_id=1, source_target_pairs={{0,16},{8,24},{16,0},{24,8},{1,17},{9,25},{17,1},{25,9},{2,18},{10... | collective-permute-start | bytes 393224 | tf_op jit(solution)/shard_map/ppermute | solution.py:152
  43.2 26.2 %collective-permute-start.4 = (f32[2,128,128]{2,1,0:T(8,128)S(1)}, f32[2,128,128]{2,1,0:T(8,128)S(1)}, u32[]{:S(2)}, u32[]{:S(2)}) collective-permute-start(f32[2,128,128]{2,1,0:T(8,128)S(1)} %get-tuple-element.70), channel_id=1, source_target_pairs={{0,24},{8,16},{16,8},{24,0},{1,25},{9,17},{17,9},{25,1},{2,26},{10... | collective-permute-start | bytes 393224 | tf_op jit(solution)/shard_map/ppermute | solution.py:152
  43.8 25.8 %collective-permute-start.17 = (f32[2,128,128]{2,1,0:T(8,128)S(1)}, f32[2,128,128]{2,1,0:T(8,128)S(1)}, u32[]{:S(2)}, u32[]{:S(2)}) collective-permute-start(f32[2,128,128]{2,1,0:T(8,128)S(1)} %get-tuple-element.62), channel_id=1, source_target_pairs={{0,8},{8,0},{16,24},{24,16},{1,9},{9,1},{17,25},{25,17},{2,10},{10... | collective-permute-start | bytes 393224 | tf_op jit(solution)/shard_map/ppermute | solution.py:152
  66.3 8.3 %collective-permute-start.18 = (f32[2,128,128]{2,1,0:T(8,128)S(1)}, f32[2,128,128]{2,1,0:T(8,128)S(1)}, u32[]{:S(2)}, u32[]{:S(2)}) collective-permute-start(f32[2,128,128]{2,1,0:T(8,128)S(1)} %get-tuple-element.64), channel_id=1, source_target_pairs={{0,16},{8,24},{16,0},{24,8},{1,17},{9,25},{17,1},{25,9},{2,18},{10... | collective-permute-start | bytes 393224 | tf_op jit(solution)/shard_map/ppermute | solution.py:152
  67.9 6.7 %collective-permute-start.19 = (f32[2,128,128]{2,1,0:T(8,128)S(1)}, f32[2,128,128]{2,1,0:T(8,128)S(1)}, u32[]{:S(2)}, u32[]{:S(2)}) collective-permute-start(f32[2,128,128]{2,1,0:T(8,128)S(1)} %get-tuple-element.63), channel_id=1, source_target_pairs={{0,24},{8,16},{16,8},{24,0},{1,25},{9,17},{17,9},{25,1},{2,26},{10... | collective-permute-start | bytes 393224 | tf_op jit(solution)/shard_map/ppermute | solution.py:152
  69.4 6.0 %collective-permute-start.9 = (f32[2,4,128,128]{3,2,1,0:T(8,128)S(1)}, f32[2,4,128,128]{3,2,1,0:T(8,128)S(1)}, u32[]{:S(2)}, u32[]{:S(2)}) collective-permute-start(f32[2,4,128,128]{3,2,1,0:T(8,128)S(1)} %add.177), channel_id=1, source_target_pairs={{0,4},{4,0},{1,5},{5,1},{2,6},{6,2},{3,7},{7,3},{8,12},{12,8},{9,1... | collective-permute-start | bytes 1572872 | tf_op jit(solution)/shard_map/ppermute | solution.py:152
  69.5 21.2 %collective-permute-start.5 = (f32[2,2,128,128]{3,2,1,0:T(8,128)S(1)}, f32[2,2,128,128]{3,2,1,0:T(8,128)S(1)}, u32[]{:S(2)}, u32[]{:S(2)}) collective-permute-start(f32[2,2,128,128]{3,2,1,0:T(8,128)S(1)} %maximum_add_fusion.4), channel_id=1, source_target_pairs={{0,2},{1,3},{2,0},{3,1},{4,6},{5,7},{6,4},{7,5},{8,10},{9,11},{10,... | collective-permute-start | bytes 786440 | tf_op jit(solution)/shard_map/ppermute | solution.py:152
  75.5 9.3 %collective-permute-start.10 = (f32[4,128,128]{2,1,0:T(8,128)S(1)}, f32[4,128,128]{2,1,0:T(8,128)S(1)}, u32[]{:S(2)}, u32[]{:S(2)}) collective-permute-start(f32[4,128,128]{2,1,0:T(8,128)S(1)} %get-tuple-element.53), channel_id=1, source_target_pairs={{0,8},{8,0},{16,24},{24,16},{1,9},{9,1},{17,25},{25,17},{2,10},{10... | collective-permute-start | bytes 786440 | tf_op jit(solution)/shard_map/ppermute | solution.py:152
  77.1 11.8 %collective-permute-start.11 = (f32[4,128,128]{2,1,0:T(8,128)S(1)}, f32[4,128,128]{2,1,0:T(8,128)S(1)}, u32[]{:S(2)}, u32[]{:S(2)}) collective-permute-start(f32[4,128,128]{2,1,0:T(8,128)S(1)} %get-tuple-element.55), channel_id=1, source_target_pairs={{0,16},{8,24},{16,0},{24,8},{1,17},{9,25},{17,1},{25,9},{2,18},{10... | collective-permute-start | bytes 786440 | tf_op jit(solution)/shard_map/ppermute | solution.py:152
  78.6 11.0 %collective-permute-start.12 = (f32[4,128,128]{2,1,0:T(8,128)S(1)}, f32[4,128,128]{2,1,0:T(8,128)S(1)}, u32[]{:S(2)}, u32[]{:S(2)}) collective-permute-start(f32[4,128,128]{2,1,0:T(8,128)S(1)} %get-tuple-element.54), channel_id=1, source_target_pairs={{0,24},{8,16},{16,8},{24,0},{1,25},{9,17},{17,9},{25,1},{2,26},{10... | collective-permute-start | bytes 786440 | tf_op jit(solution)/shard_map/ppermute | solution.py:152
  84.0 9.6 %collective-permute-start.20 = (f32[2,2,128,128]{3,2,1,0:T(8,128)S(1)}, f32[2,2,128,128]{3,2,1,0:T(8,128)S(1)}, u32[]{:S(2)}, u32[]{:S(2)}) collective-permute-start(f32[2,2,128,128]{3,2,1,0:T(8,128)S(1)} %get-tuple-element.42), channel_id=1, source_target_pairs={{0,1},{1,0},{2,3},{3,2},{4,5},{5,4},{6,7},{7,6},{8,9},{9,8},{10,11... | collective-permute-start | bytes 786440 | tf_op jit(solution)/shard_map/ppermute | solution.py:152
  90.7 16.1 %collective-permute-start.13 = (f32[2,4,128,128]{3,2,1,0:T(8,128)S(1)}, f32[2,4,128,128]{3,2,1,0:T(8,128)S(1)}, u32[]{:S(2)}, u32[]{:S(2)}) collective-permute-start(f32[2,4,128,128]{3,2,1,0:T(8,128)S(1)} %get-tuple-element.34), channel_id=1, source_target_pairs={{0,1},{1,0},{2,3},{3,2},{4,5},{5,4},{6,7},{7,6},{8,9},{9,8},{10,11... | collective-permute-start | bytes 1572872 | tf_op jit(solution)/shard_map/ppermute | solution.py:152
  91.5 28.5 %collective-permute-start.6 = (f32[2,2,128,128]{3,2,1,0:T(8,128)S(1)}, f32[2,2,128,128]{3,2,1,0:T(8,128)S(1)}, u32[]{:S(2)}, u32[]{:S(2)}) collective-permute-start(f32[2,2,128,128]{3,2,1,0:T(8,128)S(1)} %get-tuple-element.44), channel_id=1, source_target_pairs={{0,1},{1,0},{2,3},{3,2},{4,5},{5,4},{6,7},{7,6},{8,9},{9,8},{10,11... | collective-permute-start | bytes 786440 | tf_op jit(solution)/shard_map/ppermute | solution.py:152
  (5 other events, 9.0 us)

commit v2 on v0

v2 whole, which is shorter than its diff:
```python
import functools
import math

import jax
import jax.numpy as jnp
from jax import lax
from jax.experimental import pallas as pl
from jax.experimental.pallas import tpu as pltpu
from jax.sharding import PartitionSpec as P

AXES = ("sa", "sb", "sc")
CHUNKS = ((6, False), (6, False), (4, True))
SPLIT = (2,)
ORDER = (
    "pair0",
    "inner1",
    "pair2",
    "inner0",
    "total0",
    "plane2",
    "pair1",
    "plane0",
    "found2",
    "inner2",
    "state2",
    "total1",
    "plane1",
    "found0",
    "state0",
    "own0",
    "found1",
    "finish2",
    "his0",
    "state1",
    "own2",
    "his2",
    "own1",
    "his1",
)
SWAPS = (2, 1)
COSTS = {'first': 100.0, 'load': 0.001, 'inner': 0.001, 'grads': 1000.0}
VMEM = 14 * 2**20
ROWS = 128
NN = (((1,), (0,)), ((), ()))
TN = (((0,), (0,)), ((), ()))


def cost(microseconds):
    return pl.CostEstimate(flops=int(microseconds * 1e6), bytes_accessed=0, transcendentals=0)


def split(x):
    high = x.astype(jnp.bfloat16)
    low = (x - high.astype(jnp.float32)).astype(jnp.bfloat16)
    return high, low


def wide(x):
    return jnp.concatenate(split(x), axis=1)


def fold(x):
    half = x.shape[1] // 2
    return x[:, :half] + x[:, half:]


def stacked(x):
    return jnp.concatenate([x, x], axis=0)


def dot(a, b):
    return lax.dot_general(a, b, NN, preferred_element_type=jnp.float32)


def outer(a, b):
    half = a.shape[1]
    full = fold(lax.dot_general(wide(a), wide(b), TN, preferred_element_type=jnp.float32))
    return full[:half] + full[half:]


IN_VMEM = pl.BlockSpec(memory_space=pltpu.VMEM)
IN_SMEM = pl.BlockSpec(memory_space=pltpu.SMEM)
ANYWHERE = pl.BlockSpec(memory_space=pl.ANY)


def in_vmem(x):
    return pltpu.with_memory_space_constraint(x, pltpu.VMEM)


def in_hbm(x):
    return pltpu.with_memory_space_constraint(x, pltpu.HBM)


def call(kernel, out_shape, out_specs, in_specs, microseconds, name, scratch_shapes=(), aliases=None):
    return pl.pallas_call(
        kernel,
        out_shape=out_shape,
        in_specs=in_specs,
        out_specs=out_specs,
        scratch_shapes=scratch_shapes,
        input_output_aliases=aliases or {},
        compiler_params=pltpu.CompilerParams(vmem_limit_bytes=VMEM),
        cost_estimate=cost(microseconds),
        name=name,
    )


def columns_at(head, size):
    if isinstance(head, int):
        return slice(head * size, (head + 1) * size)
    return pl.ds(pl.multiple_of(head * size, size), size)


def first_kernel(place_ref, q_ref, k_ref, v_ref, g_ref, out_ref, buffers, sems):
    count, size = out_ref.shape[1], out_ref.shape[-1]
    sources = (q_ref, k_ref, v_ref, g_ref)

    def copy(j, n):
        return pltpu.make_async_copy(
            sources[n].at[:, columns_at(place_ref[1, 0] + j, size)], buffers.at[j, n], sems.at[j, n]
        )

    for j in range(count):
        for n in range(4):
            copy(j, n).start()
    for j in range(count):
        for n in range(4):
            copy(j, n).wait()
        out_ref[0, j] = outer(buffers[j, 1], buffers[j, 2])
        out_ref[1, j] = outer(buffers[j, 3], buffers[j, 0])


def first_terms(places, count, arrays, size):
    rows = arrays[0].shape[0]
    return call(
        first_kernel,
        pltpu.VMEM((2, count, size, size), jnp.float32),
        IN_VMEM,
        [IN_SMEM] + [ANYWHERE] * 4,
        COSTS["first"],
        "first_terms",
        [pltpu.VMEM((count, 4, rows, size), jnp.float32), pltpu.SemaphoreType.DMA((count, 4))],
    )(places, *map(in_hbm, arrays))


def load_kernel(place_ref, q_ref, k_ref, v_ref, g_ref, prefix_ref, suffix_ref, *rest):
    chunks = (len(rest) - 5) // 3
    owns, others, edges = rest[:chunks], (None, *rest[chunks : 2 * chunks - 1]), rest[2 * chunks - 1 : 3 * chunks - 1]
    targets, sems, edge_sems = rest[-6:-2], rest[-2], rest[-1]
    sources = (q_ref, k_ref, v_ref, g_ref)
    size = owns[0].shape[-1]
    pieces = [(n, 0, owns[n]) for n in range(chunks)] + [(n, 1, others[n]) for n in range(chunks)]
    pieces = [pieces[0]] + [p for p in pieces[1:] if p[2] is not None] + [p for p in pieces if p[2] is None]

    def copies(n, side):
        first, count = place_ref[side, n], owns[n].shape[1]
        place = pl.ds(pl.multiple_of(first * size, size), count * size)
        return [
            pltpu.make_async_copy(sources[m].at[:, place], targets[m].at[:, place], sems.at[side, n, m])
            for m in range(4)
        ]

    def edge_copies(n):
        place = pl.ds(place_ref[0, n], owns[n].shape[1])
        return [
            pltpu.make_async_copy(ref.at[place], edges[n].at[m], edge_sems.at[n, m])
            for m, ref in enumerate((prefix_ref, suffix_ref))
        ]

    for n, side, _ in pieces:
        for copy in copies(n, side):
            copy.start()
    for n in range(chunks):
        for copy in edge_copies(n):
            copy.start()
    for n, side, out_ref in pieces:
        for copy in copies(n, side):
            copy.wait()
        if out_ref is None:
            continue

        @pl.loop(0, out_ref.shape[1])
        def _(j):
            place = columns_at(place_ref[side, n] + j, size)
            q, k, v, g = (ref[:, place] for ref in targets)
            out_ref[0, j] = outer(k, v)
            out_ref[1, j] = outer(g, q)

    for n in range(chunks):
        for copy in edge_copies(n):
            copy.wait()


def load_terms(places, halves, arrays, edges, size):
    kept = pltpu.VMEM(arrays[0].shape, arrays[0].dtype)
    terms = [pltpu.VMEM((2, half, size, size), jnp.float32) for half in halves]
    chunks = len(halves)
    results = call(
        load_kernel,
        terms + terms[1:] + terms + [kept] * 4,
        [IN_VMEM] * (3 * chunks + 3),
        [IN_SMEM] + [ANYWHERE] * 6,
        COSTS["load"],
        "load_terms",
        [pltpu.SemaphoreType.DMA((2, chunks, 4)), pltpu.SemaphoreType.DMA((chunks, 2))],
    )(places, *map(in_hbm, (*arrays, *edges)))
    return results[:chunks], results[chunks : 2 * chunks - 1], results[2 * chunks - 1 : 3 * chunks - 1], results[-4:]


def inner_grads(q, k, v, g):
    count, size = len(q), q[0].shape[1]
    row = lax.broadcasted_iota(jnp.int32, (size, size), 0)
    column = lax.broadcasted_iota(jnp.int32, (size, size), 1)
    lower, upper = row >= column, row <= column

    q_t, v_t, g_t = ([wide(x.T) for x in xs] for xs in (q, v, g))
    q, k, v, g = ([wide(x) for x in xs] for xs in (q, k, v, g))
    q_rows, k_rows, g_rows = ([stacked(x) for x in xs] for xs in (q, k, g))

    before_t, after, after_t = [None], [None], [None]
    for i in range(count - 1):
        j = count - 1 - i
        before_t.append(fold(dot(v_t[i], k_rows[i])))
        after.append(fold(dot(g_t[j], q_rows[j])))
        if i > 0:
            before_t[-1] = before_t[-1] + before_t[-2]
            after[-1] = after[-1] + after[-2]
        after_t.append(after[-1].T)
    after, after_t = after[::-1], after_t[::-1]

    def scores(a, b_t, mask):
        return wide(jnp.where(mask, fold(dot(a, stacked(b_t))), 0.0))

    def both(rows, state, weights, other_rows):
        if state is None:
            return fold(dot(weights, other_rows))
        left = jnp.concatenate([rows, weights], axis=1)
        right = jnp.concatenate([stacked(wide(state)), other_rows], axis=0)
        return fold(dot(left, right))

    for i in range(count):
        yield (
            both(g[i], before_t[i], scores(g[i], v_t[i], lower), k_rows[i]),
            both(v[i], after[i], scores(v[i], g_t[i], upper), q_rows[i]),
            both(k[i], after_t[i], scores(k[i], q_t[i], upper), g_rows[i]),
        )


def blocks_of(refs, place):
    size = ROWS
    return [[ref[i : i + size, place] for i in range(0, ref.shape[0], size)] for ref in refs]


def inner_kernel(first, q_ref, k_ref, v_ref, g_ref, tie_ref, out_ref):
    size = ROWS

    @pl.loop(0, out_ref.shape[2] // size)
    def _(j):
        for i, results in enumerate(inner_grads(*blocks_of((q_ref, k_ref, v_ref, g_ref), columns_at(first + j, size)))):
            for n, x in enumerate(results):
                out_ref[n, i * size : (i + 1) * size, columns_at(j, size)] = x


def inner_terms(first, count, arrays, size, tie):
    rows = arrays[0].shape[0]
    return call(
        functools.partial(inner_kernel, first),
        pltpu.VMEM((3, rows, count * size), jnp.float32),
        IN_VMEM,
        [IN_VMEM] * 4 + [ANYWHERE],
        COSTS["inner"] * count,
        "inner_terms",
    )(*map(in_vmem, arrays), tie)


def send_kernel(make, count, size, place_ref, outs, buffer, sems):
    def copy(j, n):
        return pltpu.make_async_copy(
            buffer.at[n, :, columns_at(j, size)], outs[n].at[:, columns_at(place_ref[0] + j, size)], sems.at[j, n]
        )

    @pl.loop(0, count)
    def _(j):
        make(j)
        for n in range(3):
            copy(j, n).start()

    for j in range(count):
        for n in range(3):
            copy(j, n).wait()


def state_kernel(factor, place_ref, k_ref, v_ref, g_ref, state_ref, inner_ref, *rest):
    outs, buffer, sems = rest[-5:-2], rest[-2], rest[-1]
    count, size = state_ref.shape[1], state_ref.shape[2]

    def make(j):
        place = columns_at(place_ref[0] + j, size)
        before, after = state_ref[0, j], state_ref[1, j]
        for n, (ref, state) in enumerate(((g_ref, before.T), (v_ref, after), (k_ref, after.T))):
            x = fold(dot(wide(ref[:, place]), stacked(wide(state))))
            x = x + inner_ref[n, :, columns_at(place_ref[1] + j, size)]
            buffer[n, :, columns_at(j, size)] = (factor * x).astype(buffer.dtype)

    send_kernel(make, count, size, place_ref, outs, buffer, sems)


def grads(place, arrays, state, inner, outs, factor):
    rows, columns = arrays[0].shape
    count, size = state.shape[1], state.shape[2]
    given = [] if outs is None else list(outs)
    operands = [*arrays[1:], state, inner]
    return call(
        functools.partial(state_kernel, factor),
        [jax.ShapeDtypeStruct((rows, columns), jnp.bfloat16)] * 3,
        [ANYWHERE] * 3,
        [IN_SMEM] + [IN_VMEM] * len(operands) + [ANYWHERE] * len(given),
        COSTS["grads"] * count,
        "state_grads",
        [pltpu.VMEM((3, rows, count * size), jnp.bfloat16), pltpu.SemaphoreType.DMA((count, 3))],
        {1 + len(operands) + n: n for n in range(len(given))},
    )(place, *map(in_vmem, operands), *given)


def swap(x, axis, offset, name):
    with jax.named_scope(name):
        return lax.ppermute(x, axis, [(i, i ^ offset) for i in range(lax.axis_size(axis))])


def pick(low, lower, upper):
    return jnp.where(low, lower, 0.0), jnp.where(low, 0.0, upper)


class Order:
    def __init__(self):
        self.last = None

    def then(self, x):
        if self.last is None:
            return x
        return lax.optimization_barrier((x, self.last))[0]

    def did(self, x):
        self.last = x
        return x


def shards(queries, key_rows, value_rows, out_grad, prefix_state, suffix_state):
    rows = queries.shape[0]
    heads, size = prefix_state.shape[:2]
    sizes = [lax.axis_size(axis) for axis in AXES]
    factor = 1.0 / math.sqrt(size * rows * math.prod(sizes))
    a, b, c = (lax.axis_index(axis) for axis in AXES)
    odd = c % 2
    upper = odd == 1
    arrays = (queries, key_rows, value_rows, out_grad)
    offsets = range(2, sizes[2], 2)
    chunks = range(len(CHUNKS))
    starts = [sum(count for count, _ in CHUNKS[:n]) for n in chunks]
    halves = [count // 2 for count, _ in CHUNKS]
    own = [start + odd * half for start, half in zip(starts, halves)]
    his = [start + (1 - odd) * half for start, half in zip(starts, halves)]
    pairs = {k: (c ^ k) < c for k in offsets}
    chips = {k: (b ^ k) < b for k in range(1, sizes[1])}
    faces = {k: (a ^ k) < a for k in range(1, sizes[0])}
    sides = jnp.stack([jnp.stack(own), jnp.stack(his)]).astype(jnp.int32)
    places = [
        [jnp.stack([first[n], first[n] - starts[n]]).astype(jnp.int32) for n in chunks] for first in (own, his)
    ]
    upper, pairs, chips, faces, sides, places = lax.optimization_barrier((upper, pairs, chips, faces, sides, places))
    order = Order()
    then, did = order.then, order.did

    first = did(first_terms(sides, halves[0], arrays, size))
    received = {0: swap(first, "sc", 1, "swap0")}
    mine, given, edge, arrays = load_terms(then(sides), halves, arrays, (prefix_state, suffix_state), size)
    did(mine[0])
    for n in SWAPS:
        received[n] = swap(given[n - 1], "sc", 1, f"swap{n}")
    total, found, waiting, extra, state, inners, results, outs = {}, {}, {}, {}, {}, {}, {}, [None]

    def both(low, lower, upper):
        return jnp.stack(pick(low, lower, upper))

    def pair(n):
        total[n] = did(mine[n] + then(received[n]))
        found[n] = edge[n]
        if not CHUNKS[n][1]:
            waiting[n] = [(pairs[k], swap(total[n], "sc", k, f"middle{n}")) for k in offsets]

    def total_(n):
        for low, other in waiting[n]:
            other = then(other)
            total[n] = total[n] + other
            found[n] = found[n] + both(low, other[0], other[1])
        did(total[n])

    def plane(n):
        x = then(total[n])
        waiting[n] = [(faces[k], swap(jnp.where(faces[k], x[1], x[0]), "sa", k, f"plane{n}")) for k in faces]

    def found_(n):
        x = 0.0
        for low, other in waiting[n]:
            other = then(other)
            x = x + both(low, other, other)
        extra[n] = did(x)
        waiting[n] = []
        for k in chips:
            down, up = pick(chips[k], total[n][1], total[n][0])
            if n in SPLIT:
                waiting[n].append([swap(x[0] + up, "sb", k, f"core{n}"), swap(x[1] + down, "sb", k, f"core{n}")])
            else:
                waiting[n].append([swap(x + jnp.stack([up, down]), "sb", k, f"core{n}")])

    def hand_back(n):
        theirs = then(received[n])
        state[n, 0] = state[n, 0] + found[n]
        state_his = did(state[n, 0] + jnp.stack(pick(upper, mine[n][1], mine[n][0])[::-1]))
        state[n, 0] = state[n, 0] + both(upper, theirs[0], theirs[1])
        state[n, 1] = swap(state_his, "sc", 1, f"back{n}")

    def state_(n):
        x = extra[n]
        for others in waiting[n]:
            others = [then(other) for other in others]
            x = x + (others[0] if len(others) == 1 else jnp.stack(others))
        state[n, 0] = x
        if not CHUNKS[n][1]:
            return hand_back(n)
        did(x)
        waiting[n] = []
        for k in offsets:
            down, up = pick(pairs[k], total[n][1], total[n][0])
            waiting[n].append(swap(x + jnp.stack([up, down]), "sc", k, f"middle{n}"))

    def finish(n):
        for other in waiting[n]:
            state[n, 0] = state[n, 0] + then(other)
        hand_back(n)

    def inner(n):
        inners[n] = did(inner_terms(starts[n], 2 * halves[n], arrays, size, order.last))

    def result(side, n):
        place = then(places[side][n])
        outs[0] = grads(place, arrays, then(state[n, side]), inners[n], outs[0], factor)
        did(outs[0])

    steps = {
        "pair": pair,
        "total": total_,
        "plane": plane,
        "found": found_,
        "state": state_,
        "finish": finish,
        "inner": inner,
        "own": functools.partial(result, 0),
        "his": functools.partial(result, 1),
    }
    for step in ORDER:
        steps[step[:-1]](int(step[-1]))
    return tuple(outs[0])


def solution(mesh):
    rows = P(AXES, None)
    return jax.shard_map(
        shards,
        mesh=mesh,
        in_specs=(rows, rows, rows, rows, P(), P()),
        out_specs=(rows, rows, rows),
        check_vma=False,
    )
```

time: 542 us -> 99.2 us (0.18); the launches traced: 536 us -> 99 us
  waiting for transfers between devices: 363 us -> 20 us
  matrix products: 127 us -> 0 us
  Pallas kernels: 0 us -> 48.7 us
  starting transfers between devices: 0.27 us -> 27.3 us
  local copies, waits for them, and re-layouts: 26.4 us -> 0 us
  between operations: 16 us -> 1.04 us
    all_gather x6 -> x0, waiting for transfers between devices: 209 us -> none  [entering(): gathered = jax.tree.map(lambda a: lax.all_gather(a, axis), part)]
    psum x3 -> x0, waiting for transfers between devices: 150 us -> none  [the longest x1 88.6 us: run_chain(): group_sum = lax.psum((local_terms[0], local_terms[1]), 'sc')]
    dot_general x10 -> x0, matrix products: 127 us -> none  [the longest x1 21.3 us: shards(): jnp.einsum('hts,shd->thd', grad_scores, key_t, precision=highest)]
    pallas_call x0 -> x11, Pallas kernels: none -> 48.7 us  [the longest x3 21.9 us: inner_terms(): call(functools.partial(inner_kernel, first), pltpu.VMEM((3, rows, count *...]
    ppermute x0 -> x22, starting transfers between devices: none -> 27.3 us  [swap(): lax.ppermute(x, axis, [(i, i ^ offset) for i in range(lax.axis_size(axis))])]
    ppermute x0 -> x22, waiting for transfers between devices: none -> 20 us  [swap(): lax.ppermute(x, axis, [(i, i ^ offset) for i in range(lax.axis_size(axis))])]
    unnamed x22 -> x0, local copies, waits for them, and re-layouts: 19 us -> none
    reshape x1 -> x0, local copies, waits for them, and re-layouts: 5.88 us -> none  [shards(): grad_t = out_grad.reshape(shaped)]
  transfers between devices with their start and end apart: 9 -> 22, of which waited for: 9 -> 9; matrix products, arithmetic and copies ran while one was open for 17% -> 2% of each run, Pallas kernels for 0% -> 43%
where the time goes in v2:
time: 99.2 us; the launch traced here: 99 us
  Pallas kernels  48.7 us (49%)
  starting transfers between devices  27.3 us (28%)
  waiting for transfers between devices  20 us (20%)
  other arithmetic  2.08 us (2%)
  between operations  1.04 us (1%)
    ppermute x22, starting transfers between devices, swap(): lax.ppermute(x, axis, [(i, i ^ offset) for i in range(lax.axis_size(axis))])  27.3 us
    pallas_call x3, Pallas kernels, inner_terms(): call(functools.partial(inner_kernel, first), pltpu.VMEM((3, rows, count *...  21.9 us
    ppermute x22, waiting for transfers between devices, swap(): lax.ppermute(x, axis, [(i, i ^ offset) for i in range(lax.axis_size(axis))])  20 us
    pallas_call x6, Pallas kernels, grads(): call(functools.partial(state_kernel, factor), [jax.ShapeDtypeStruct((rows...  15.8 us
    pallas_call x1, Pallas kernels, load_terms(): call(load_kernel, terms + terms[1:] + terms + [kept] * 4, [IN_VMEM] * (3...  8.07 us
    pallas_call x1, Pallas kernels, first_terms(): call(first_kernel, pltpu.VMEM((2, count, size, size), jnp.float32), IN_VM...  2.94 us
  transfers between devices with their start and end apart: 22, of which 9 were waited for; matrix products, arithmetic and copies ran while one was open for 2% of the time, Pallas kernels for 43%

profile of v2, /device:TPU:0, one launch (start us, length us, event | category | flops | bytes accessed | tf_op | source)
XLA Modules:
  0.0 99.0 jit_solution(5597407385253386522)
XLA Ops:
  1.0 2.9 %first_terms.1 = f32[2,3,128,128]{3,2,1,0:T(8,128)S(1)} custom-call(s32[2,3]{1,0:T(2,128)S(1)} %pad_add_fusion.place_ref, f32[512,2048]{1,0:T(8,128)} %q_ref.3, f32[512,2048]{1,0:T(8,128)} %k_ref.3, f32[512,2048]{1,0:T(8,128)} %v_ref.3, f32[512,2048]{1,0:T(8,128)} %g_ref.3), custom_call_target="tpu_custom_call" | custom-call | flops 100000000 | tf_op jit(solution)/shard_map/first_terms/pallas_call | solution.py:135
  3.9 3.1 %collective-permute-start.1 = (f32[2,3,128,128]{3,2,1,0:T(8,128)S(1)}, f32[2,3,128,128]{3,2,1,0:T(8,128)S(1)}, u32[]{:S(2)}, u32[]{:S(2)}) collective-permute-start(f32[2,3,128,128]{3,2,1,0:T(8,128)S(1)} %first_terms.1), channel_id=1, source_target_pairs={{0,1},{1,0},{2,3},{3,2},{4,5},{5,4},{6,7},{7,6},{8,9},{9,8},{10,11... | collective-permute-start | bytes 1179656 | tf_op jit(solution)/shard_map/swap0/ppermute | solution.py:327
  7.0 8.1 %load_terms.1 = (f32[2,3,128,128]{3,2,1,0:T(8,128)S(1)}, f32[2,3,128,128]{3,2,1,0:T(8,128)S(1)}, f32[2,2,128,128]{3,2,1,0:T(8,128)S(1)}, f32[2,3,128,128]{3,2,1,...) custom-call(s32[2,3]{1,0:T(2,128)S(1)} %pad_add_fusion.place_ref, ...), custom_call_target="tpu_custom_call" | custom-call | flops 1000 | tf_op jit(solution)/shard_map/load_terms/pallas_call | solution.py:198
  15.2 2.0 %collective-permute-start = (f32[2,3,128,128]{3,2,1,0:T(8,128)S(1)}, f32[2,3,128,128]{3,2,1,0:T(8,128)S(1)}, u32[]{:S(2)}, u32[]{:S(2)}) collective-permute-start(f32[2,3,128,128]{3,2,1,0:T(8,128)S(1)} %get-tuple-element.89), channel_id=1, source_target_pairs={{0,1},{1,0},{2,3},{3,2},{4,5},{5,4},{6,7},{7,6},{8,9},{9,8},{10,11... | collective-permute-start | bytes 1179656 | tf_op jit(solution)/shard_map/swap1/ppermute | solution.py:327
  17.3 2.7 %collective-permute-start.2 = (f32[2,3,128,128]{3,2,1,0:T(8,128)S(1)}, f32[2,3,128,128]{3,2,1,0:T(8,128)S(1)}, u32[]{:S(2)}, u32[]{:S(2)}) collective-permute-start(f32[2,3,128,128]{3,2,1,0:T(8,128)S(1)} %add.132.tie_ref), channel_id=1, source_target_pairs={{0,2},{1,3},{2,0},{3,1},{4,6},{5,7},{6,4},{7,5},{8,10},{9,11},{10,... | collective-permute-start | bytes 1179656 | tf_op jit(solution)/shard_map/middle0/ppermute | solution.py:327
  20.0 8.2 %inner_terms.3.inner_ref = f32[3,512,768]{2,1,0:T(8,128)S(1)} custom-call(f32[512,2048]{1,0:T(8,128)S(1)} %get-tuple-element.92.q_ref, f32[512,2048]{1,0:T(8,128)S(1)} %get-tuple-element.93.k_ref, f32[512,2048]{1,0:T(8,128)S(1)} %get-tuple-element.94.v_ref, f32[512,2048]{1,0:T(8,128)S(1)} %get-tuple-element.95.g_ref, f32[2,3,128,128]{3,2,1,0:T(8,128)S(1)} %add.132.tie_ref), custom_call_target="tpu_custom_call" | custom-call | flops 6000 | tf_op jit(solution)/shard_map/inner_terms/pallas_call | solution.py:266
  28.2 4.6 %collective-permute-done.3 = f32[2,2,128,128]{3,2,1,0:T(8,128)S(1)} collective-permute-done((f32[2,2,128,128]{3,2,1,0:T(8,128)S(1)}, f32[2,2,128,128]{3,2,1,0:T(8,128)S(1)}, u32[]{:S(2)}, u32[]{:S(2)}) %collective-permute-start.3) | collective-permute-done | bytes 262176 | tf_op jit(solution)/shard_map/swap2/ppermute | solution.py:327
  32.9 8.2 %inner_terms.4.inner_ref = f32[3,512,768]{2,1,0:T(8,128)S(1)} custom-call(f32[512,2048]{1,0:T(8,128)S(1)} %get-tuple-element.92.q_ref, f32[512,2048]{1,0:T(8,128)S(1)} %get-tuple-element.93.k_ref, f32[512,2048]{1,0:T(8,128)S(1)} %get-tuple-element.94.v_ref, f32[512,2048]{1,0:T(8,128)S(1)} %get-tuple-element.95.g_ref, f32[2,2,128,128]{3,2,1,0:T(8,128)S(1)} %add.133.tie_ref), custom_call_target="tpu_custom_call" | custom-call | flops 6000 | tf_op jit(solution)/shard_map/inner_terms/pallas_call | solution.py:266
  41.8 2.5 %collective-permute-start.7 = (f32[2,128,128]{2,1,0:T(8,128)S(1)}, f32[2,128,128]{2,1,0:T(8,128)S(1)}, u32[]{:S(2)}, u32[]{:S(2)}) collective-permute-start(f32[2,128,128]{2,1,0:T(8,128)S(1)} %get-tuple-element.199), channel_id=1, source_target_pairs={{0,24},{8,16},{16,8},{24,0},{1,25},{9,17},{17,9},{25,1},{2,26},{10... | collective-permute-start | bytes 393224 | tf_op jit(solution)/shard_map/plane2/ppermute | solution.py:327
  47.0 2.2 %collective-permute-done.7 = f32[2,128,128]{2,1,0:T(8,128)S(1)} collective-permute-done((f32[2,128,128]{2,1,0:T(8,128)S(1)}, f32[2,128,128]{2,1,0:T(8,128)S(1)}, u32[]{:S(2)}, u32[]{:S(2)}) %collective-permute-start.7) | collective-permute-done | bytes 131104 | tf_op jit(solution)/shard_map/plane2/ppermute | solution.py:327
  49.2 2.5 %collective-permute-start.13 = (f32[3,128,128]{2,1,0:T(8,128)S(1)}, f32[3,128,128]{2,1,0:T(8,128)S(1)}, u32[]{:S(2)}, u32[]{:S(2)}) collective-permute-start(f32[3,128,128]{2,1,0:T(8,128)S(1)} %get-tuple-element.189), channel_id=1, source_target_pairs={{0,24},{8,16},{16,8},{24,0},{1,25},{9,17},{17,9},{25,1},{2,26},{10... | collective-permute-start | bytes 589832 | tf_op jit(solution)/shard_map/plane0/ppermute | solution.py:327
  52.9 5.5 %inner_terms.5.inner_ref = f32[3,512,512]{2,1,0:T(8,128)S(1)} custom-call(f32[512,2048]{1,0:T(8,128)S(1)} %get-tuple-element.92.q_ref, f32[512,2048]{1,0:T(8,128)S(1)} %get-tuple-element.93.k_ref, f32[512,2048]{1,0:T(8,128)S(1)} %get-tuple-element.94.v_ref, f32[512,2048]{1,0:T(8,128)S(1)} %get-tuple-element.95.g_ref, f32[2,2,128,128]{3,2,1,0:T(8,128)S(1)} %fusion.4.tie_ref), custom_call_target="tpu_custom_call" | custom-call | flops 4000 | tf_op jit(solution)/shard_map/inner_terms/pallas_call | solution.py:266
  59.0 2.7 %collective-permute-start.18 = (f32[2,2,128,128]{3,2,1,0:T(8,128)S(1)}, f32[2,2,128,128]{3,2,1,0:T(8,128)S(1)}, u32[]{:S(2)}, u32[]{:S(2)}) collective-permute-start(f32[2,2,128,128]{3,2,1,0:T(8,128)S(1)} %get-tuple-element.161), channel_id=1, source_target_pairs={{0,2},{1,3},{2,0},{3,1},{4,6},{5,7},{6,4},{7,5},{8,10},{9,11},{10,... | collective-permute-start | bytes 786440 | tf_op jit(solution)/shard_map/middle2/ppermute | solution.py:327
  61.8 1.6 %collective-permute-start.10 = (f32[3,128,128]{2,1,0:T(8,128)S(1)}, f32[3,128,128]{2,1,0:T(8,128)S(1)}, u32[]{:S(2)}, u32[]{:S(2)}) collective-permute-start(f32[3,128,128]{2,1,0:T(8,128)S(1)} %get-tuple-element.179), channel_id=1, source_target_pairs={{0,8},{8,0},{16,24},{24,16},{1,9},{9,1},{17,25},{25,17},{2,10},{10... | collective-permute-start | bytes 589832 | tf_op jit(solution)/shard_map/plane1/ppermute | solution.py:327
  65.9 1.6 %collective-permute-done.14 = f32[2,3,128,128]{3,2,1,0:T(8,128)S(1)} collective-permute-done((f32[2,3,128,128]{3,2,1,0:T(8,128)S(1)}, f32[2,3,128,128]{3,2,1,0:T(8,128)S(1)}, u32[]{:S(2)}, u32[]{:S(2)}) %collective-permute-start.14) | collective-permute-done | bytes 393248 | tf_op jit(solution)/shard_map/core0/ppermute | solution.py:327
  67.8 2.3 %collective-permute-start.19 = (f32[2,3,128,128]{3,2,1,0:T(8,128)S(1)}, f32[2,3,128,128]{3,2,1,0:T(8,128)S(1)}, u32[]{:S(2)}, u32[]{:S(2)}) collective-permute-start(f32[2,3,128,128]{3,2,1,0:T(8,128)S(1)} %maximum_add_fusion.3), channel_id=1, source_target_pairs={{0,1},{1,0},{2,3},{3,2},{4,5},{5,4},{6,7},{7,6},{8,9},{9,8},{10,11... | collective-permute-start | bytes 1179656 | tf_op jit(solution)/shard_map/back0/ppermute | solution.py:327
  70.0 2.8 %state_grads.6 = (bf16[512,2048]{1,0:T(8,128)(2,1)}, bf16[512,2048]{1,0:T(8,128)(2,1)}, bf16[512,2048]{1,0:T(8,128)(2,1)}) custom-call(s32[2]{0:T(128)S(1)} %get-tuple-element.121.place_ref, f32[512,2048]{1,0:T(8,128)S(1)} %get-tuple-element.93.k_ref, f32[512,2048]{1,0:T(8,128)S(1)} %get-tuple-element.94.v_ref, f32[512,2048]{1,0:T(8,128)S(1)} %get-tuple-element.95.g_ref, ...), custom_call_target="tpu_custom_call" | custom-call | flops 3000000000 | tf_op jit(solution)/shard_map/state_grads/pallas_call | solution.py:313
  76.6 5.4 %collective-permute-done.19.state_ref = f32[2,3,128,128]{3,2,1,0:T(8,128)S(1)} collective-permute-done((f32[2,3,128,128]{3,2,1,0:T(8,128)S(1)}, f32[2,3,128,128]{3,2,1,0:T(8,128)S(1)}, u32[]{:S(2)}, u32[]{:S(2)}) %collective-permute-start.19) | collective-permute-done | bytes 393248 | tf_op jit(solution)/shard_map/back0/ppermute | solution.py:327
  82.1 2.8 %state_grads.7 = (bf16[512,2048]{1,0:T(8,128)(2,1)}, bf16[512,2048]{1,0:T(8,128)(2,1)}, bf16[512,2048]{1,0:T(8,128)(2,1)}) custom-call(s32[2]{0:T(128)S(1)} %get-tuple-element.133.place_ref, f32[512,2048]{1,0:T(8,128)S(1)} %get-tuple-element.93.k_ref, ...), custom_call_target="tpu_custom_call", output_to_operand_aliasing={{0}: (6, {}), {1}: (7, {}), {2}: (8, {})} | custom-call | flops 3000000000 | tf_op jit(solution)/shard_map/state_grads/pallas_call | solution.py:313
  85.2 2.3 %state_grads.8 = (bf16[512,2048]{1,0:T(8,128)(2,1)}, bf16[512,2048]{1,0:T(8,128)(2,1)}, bf16[512,2048]{1,0:T(8,128)(2,1)}) custom-call(s32[2]{0:T(128)S(1)} %get-tuple-element.140.place_ref, f32[512,2048]{1,0:T(8,128)S(1)} %get-tuple-element.93.k_ref, ...), custom_call_target="tpu_custom_call", output_to_operand_aliasing={{0}: (6, {}), {1}: (7, {}), {2}: (8, {})} | custom-call | flops 2000000000 | tf_op jit(solution)/shard_map/state_grads/pallas_call | solution.py:313
  87.7 2.3 %state_grads.9 = (bf16[512,2048]{1,0:T(8,128)(2,1)}, bf16[512,2048]{1,0:T(8,128)(2,1)}, bf16[512,2048]{1,0:T(8,128)(2,1)}) custom-call(s32[2]{0:T(128)S(1)} %get-tuple-element.146.place_ref, f32[512,2048]{1,0:T(8,128)S(1)} %get-tuple-element.93.k_ref, ...), custom_call_target="tpu_custom_call", output_to_operand_aliasing={{0}: (6, {}), {1}: (7, {}), {2}: (8, {})} | custom-call | flops 2000000000 | tf_op jit(solution)/shard_map/state_grads/pallas_call | solution.py:313
  89.9 2.8 %state_grads.10 = (bf16[512,2048]{1,0:T(8,128)(2,1)}, bf16[512,2048]{1,0:T(8,128)(2,1)}, bf16[512,2048]{1,0:T(8,128)(2,1)}) custom-call(s32[2]{0:T(128)S(1)} %get-tuple-element.151.place_ref, f32[512,2048]{1,0:T(8,128)S(1)} %get-tuple-element.93.k_ref, ...), custom_call_target="tpu_custom_call", output_to_operand_aliasing={{0}: (6, {}), {1}: (7, {}), {2}: (8, {})} | custom-call | flops 3000000000 | tf_op jit(solution)/shard_map/state_grads/pallas_call | solution.py:313
  92.8 3.5 %collective-permute-done.21.state_ref = f32[2,3,128,128]{3,2,1,0:T(8,128)S(1)} collective-permute-done((f32[2,3,128,128]{3,2,1,0:T(8,128)S(1)}, f32[2,3,128,128]{3,2,1,0:T(8,128)S(1)}, u32[]{:S(2)}, u32[]{:S(2)}) %collective-permute-start.21) | collective-permute-done | bytes 393248 | tf_op jit(solution)/shard_map/back1/ppermute | solution.py:327
  96.2 2.8 %state_grads.11 = (bf16[512,2048]{1,0:T(8,128)(2,1)}, bf16[512,2048]{1,0:T(8,128)(2,1)}, bf16[512,2048]{1,0:T(8,128)(2,1)}) custom-call(s32[2]{0:T(128)S(1)} %get-tuple-element.157.place_ref, f32[512,2048]{1,0:T(8,128)S(1)} %get-tuple-element.93.k_ref, ...), custom_call_target="tpu_custom_call", output_to_operand_aliasing={{0}: (6, {}), {1}: (7, {}), {2}: (8, {})} | custom-call | flops 3000000000 | tf_op jit(solution)/shard_map/state_grads/pallas_call | solution.py:313
  (73 shorter events, 12.7 us)
Async XLA Ops:
  3.9 13.3 %collective-permute-start.1 = (f32[2,3,128,128]{3,2,1,0:T(8,128)S(1)}, f32[2,3,128,128]{3,2,1,0:T(8,128)S(1)}, u32[]{:S(2)}, u32[]{:S(2)}) collective-permute-start(f32[2,3,128,128]{3,2,1,0:T(8,128)S(1)} %first_terms.1), channel_id=1, source_target_pairs={{0,1},{1,0},{2,3},{3,2},{4,5},{5,4},{6,7},{7,6},{8,9},{9,8},{10,11... | collective-permute-start | bytes 1179656 | tf_op jit(solution)/shard_map/swap0/ppermute | solution.py:327
  15.1 17.7 %collective-permute-start.3 = (f32[2,2,128,128]{3,2,1,0:T(8,128)S(1)}, f32[2,2,128,128]{3,2,1,0:T(8,128)S(1)}, u32[]{:S(2)}, u32[]{:S(2)}) collective-permute-start(f32[2,2,128,128]{3,2,1,0:T(8,128)S(1)} %get-tuple-element.97), channel_id=1, source_target_pairs={{0,1},{1,0},{2,3},{3,2},{4,5},{5,4},{6,7},{7,6},{8,9},{9,8},{10,11... | collective-permute-start | bytes 786440 | tf_op jit(solution)/shard_map/swap2/ppermute | solution.py:327
  15.2 26.0 %collective-permute-start = (f32[2,3,128,128]{3,2,1,0:T(8,128)S(1)}, f32[2,3,128,128]{3,2,1,0:T(8,128)S(1)}, u32[]{:S(2)}, u32[]{:S(2)}) collective-permute-start(f32[2,3,128,128]{3,2,1,0:T(8,128)S(1)} %get-tuple-element.89), channel_id=1, source_target_pairs={{0,1},{1,0},{2,3},{3,2},{4,5},{5,4},{6,7},{7,6},{8,9},{9,8},{10,11... | collective-permute-start | bytes 1179656 | tf_op jit(solution)/shard_map/swap1/ppermute | solution.py:327
  17.3 23.8 %collective-permute-start.2 = (f32[2,3,128,128]{3,2,1,0:T(8,128)S(1)}, f32[2,3,128,128]{3,2,1,0:T(8,128)S(1)}, u32[]{:S(2)}, u32[]{:S(2)}) collective-permute-start(f32[2,3,128,128]{3,2,1,0:T(8,128)S(1)} %add.132.tie_ref), channel_id=1, source_target_pairs={{0,2},{1,3},{2,0},{3,1},{4,6},{5,7},{6,4},{7,5},{8,10},{9,11},{10,... | collective-permute-start | bytes 1179656 | tf_op jit(solution)/shard_map/middle0/ppermute | solution.py:327
  41.2 20.5 %collective-permute-start.4 = (f32[2,3,128,128]{3,2,1,0:T(8,128)S(1)}, f32[2,3,128,128]{3,2,1,0:T(8,128)S(1)}, u32[]{:S(2)}, u32[]{:S(2)}) collective-permute-start(f32[2,3,128,128]{3,2,1,0:T(8,128)S(1)} %add.135), channel_id=1, source_target_pairs={{0,2},{1,3},{2,0},{3,1},{4,6},{5,7},{6,4},{7,5},{8,10},{9,11},{10,... | collective-permute-start | bytes 1179656 | tf_op jit(solution)/shard_map/middle1/ppermute | solution.py:327
  41.8 7.4 %collective-permute-start.7 = (f32[2,128,128]{2,1,0:T(8,128)S(1)}, f32[2,128,128]{2,1,0:T(8,128)S(1)}, u32[]{:S(2)}, u32[]{:S(2)}) collective-permute-start(f32[2,128,128]{2,1,0:T(8,128)S(1)} %get-tuple-element.199), channel_id=1, source_target_pairs={{0,24},{8,16},{16,8},{24,0},{1,25},{9,17},{17,9},{25,1},{2,26},{10... | collective-permute-start | bytes 393224 | tf_op jit(solution)/shard_map/plane2/ppermute | solution.py:327
  44.4 7.8 %collective-permute-start.5 = (f32[2,128,128]{2,1,0:T(8,128)S(1)}, f32[2,128,128]{2,1,0:T(8,128)S(1)}, u32[]{:S(2)}, u32[]{:S(2)}) collective-permute-start(f32[2,128,128]{2,1,0:T(8,128)S(1)} %get-tuple-element.200), channel_id=1, source_target_pairs={{0,8},{8,0},{16,24},{24,16},{1,9},{9,1},{17,25},{25,17},{2,10},{10... | collective-permute-start | bytes 393224 | tf_op jit(solution)/shard_map/plane2/ppermute | solution.py:327
  44.9 7.2 %collective-permute-start.6 = (f32[2,128,128]{2,1,0:T(8,128)S(1)}, f32[2,128,128]{2,1,0:T(8,128)S(1)}, u32[]{:S(2)}, u32[]{:S(2)}) collective-permute-start(f32[2,128,128]{2,1,0:T(8,128)S(1)} %get-tuple-element.201), channel_id=1, source_target_pairs={{0,16},{8,24},{16,0},{24,8},{1,17},{9,25},{17,1},{25,9},{2,18},{10... | collective-permute-start | bytes 393224 | tf_op jit(solution)/shard_map/plane2/ppermute | solution.py:327
  45.4 18.0 %collective-permute-start.11 = (f32[3,128,128]{2,1,0:T(8,128)S(1)}, f32[3,128,128]{2,1,0:T(8,128)S(1)}, u32[]{:S(2)}, u32[]{:S(2)}) collective-permute-start(f32[3,128,128]{2,1,0:T(8,128)S(1)} %get-tuple-element.188), channel_id=1, source_target_pairs={{0,8},{8,0},{16,24},{24,16},{1,9},{9,1},{17,25},{25,17},{2,10},{10... | collective-permute-start | bytes 589832 | tf_op jit(solution)/shard_map/plane0/ppermute | solution.py:327
  49.2 15.6 %collective-permute-start.13 = (f32[3,128,128]{2,1,0:T(8,128)S(1)}, f32[3,128,128]{2,1,0:T(8,128)S(1)}, u32[]{:S(2)}, u32[]{:S(2)}) collective-permute-start(f32[3,128,128]{2,1,0:T(8,128)S(1)} %get-tuple-element.189), channel_id=1, source_target_pairs={{0,24},{8,16},{16,8},{24,0},{1,25},{9,17},{17,9},{25,1},{2,26},{10... | collective-permute-start | bytes 589832 | tf_op jit(solution)/shard_map/plane0/ppermute | solution.py:327
  52.3 6.1 %collective-permute-start.8 = (f32[2,128,128]{2,1,0:T(8,128)S(1)}, f32[2,128,128]{2,1,0:T(8,128)S(1)}, u32[]{:S(2)}, u32[]{:S(2)}) collective-permute-start(f32[2,128,128]{2,1,0:T(8,128)S(1)} %get-tuple-element.171), channel_id=1, source_target_pairs={{0,4},{4,0},{1,5},{5,1},{2,6},{6,2},{3,7},{7,3},{8,12},{12,8},{9,1... | collective-permute-start | bytes 393224 | tf_op jit(solution)/shard_map/core2/ppermute | solution.py:327
  52.4 6.5 %collective-permute-start.9 = (f32[2,128,128]{2,1,0:T(8,128)S(1)}, f32[2,128,128]{2,1,0:T(8,128)S(1)}, u32[]{:S(2)}, u32[]{:S(2)}) collective-permute-start(f32[2,128,128]{2,1,0:T(8,128)S(1)} %get-tuple-element.172), channel_id=1, source_target_pairs={{0,4},{4,0},{1,5},{5,1},{2,6},{6,2},{3,7},{7,3},{8,12},{12,8},{9,1... | collective-permute-start | bytes 393224 | tf_op jit(solution)/shard_map/core2/ppermute | solution.py:327
  58.4 7.2 %collective-permute-start.12 = (f32[3,128,128]{2,1,0:T(8,128)S(1)}, f32[3,128,128]{2,1,0:T(8,128)S(1)}, u32[]{:S(2)}, u32[]{:S(2)}) collective-permute-start(f32[3,128,128]{2,1,0:T(8,128)S(1)} %get-tuple-element.190), channel_id=1, source_target_pairs={{0,16},{8,24},{16,0},{24,8},{1,17},{9,25},{17,1},{25,9},{2,18},{10... | collective-permute-start | bytes 589832 | tf_op jit(solution)/shard_map/plane0/ppermute | solution.py:327
  59.0 16.1 %collective-permute-start.18 = (f32[2,2,128,128]{3,2,1,0:T(8,128)S(1)}, f32[2,2,128,128]{3,2,1,0:T(8,128)S(1)}, u32[]{:S(2)}, u32[]{:S(2)}) collective-permute-start(f32[2,2,128,128]{3,2,1,0:T(8,128)S(1)} %get-tuple-element.161), channel_id=1, source_target_pairs={{0,2},{1,3},{2,0},{3,1},{4,6},{5,7},{6,4},{7,5},{8,10},{9,11},{10,... | collective-permute-start | bytes 786440 | tf_op jit(solution)/shard_map/middle2/ppermute | solution.py:327
  61.8 13.1 %collective-permute-start.10 = (f32[3,128,128]{2,1,0:T(8,128)S(1)}, f32[3,128,128]{2,1,0:T(8,128)S(1)}, u32[]{:S(2)}, u32[]{:S(2)}) collective-permute-start(f32[3,128,128]{2,1,0:T(8,128)S(1)} %get-tuple-element.179), channel_id=1, source_target_pairs={{0,8},{8,0},{16,24},{24,16},{1,9},{9,1},{17,25},{25,17},{2,10},{10... | collective-permute-start | bytes 589832 | tf_op jit(solution)/shard_map/plane1/ppermute | solution.py:327
  63.4 9.9 %collective-permute-start.16 = (f32[3,128,128]{2,1,0:T(8,128)S(1)}, f32[3,128,128]{2,1,0:T(8,128)S(1)}, u32[]{:S(2)}, u32[]{:S(2)}) collective-permute-start(f32[3,128,128]{2,1,0:T(8,128)S(1)} %get-tuple-element.180), channel_id=1, source_target_pairs={{0,24},{8,16},{16,8},{24,0},{1,25},{9,17},{17,9},{25,1},{2,26},{10... | collective-permute-start | bytes 589832 | tf_op jit(solution)/shard_map/plane1/ppermute | solution.py:327
  64.9 10.0 %collective-permute-start.15 = (f32[3,128,128]{2,1,0:T(8,128)S(1)}, f32[3,128,128]{2,1,0:T(8,128)S(1)}, u32[]{:S(2)}, u32[]{:S(2)}) collective-permute-start(f32[3,128,128]{2,1,0:T(8,128)S(1)} %get-tuple-element.181), channel_id=1, source_target_pairs={{0,16},{8,24},{16,0},{24,8},{1,17},{9,25},{17,1},{25,9},{2,18},{10... | collective-permute-start | bytes 589832 | tf_op jit(solution)/shard_map/plane1/ppermute | solution.py:327
  65.8 1.8 %collective-permute-start.14 = (f32[2,3,128,128]{3,2,1,0:T(8,128)S(1)}, f32[2,3,128,128]{3,2,1,0:T(8,128)S(1)}, u32[]{:S(2)}, u32[]{:S(2)}) collective-permute-start(f32[2,3,128,128]{3,2,1,0:T(8,128)S(1)} %get-tuple-element.167), channel_id=1, source_target_pairs={{0,4},{4,0},{1,5},{5,1},{2,6},{6,2},{3,7},{7,3},{8,12},{12,8},{9,1... | collective-permute-start | bytes 1179656 | tf_op jit(solution)/shard_map/core0/ppermute | solution.py:327
  67.8 14.3 %collective-permute-start.19 = (f32[2,3,128,128]{3,2,1,0:T(8,128)S(1)}, f32[2,3,128,128]{3,2,1,0:T(8,128)S(1)}, u32[]{:S(2)}, u32[]{:S(2)}) collective-permute-start(f32[2,3,128,128]{3,2,1,0:T(8,128)S(1)} %maximum_add_fusion.3), channel_id=1, source_target_pairs={{0,1},{1,0},{2,3},{3,2},{4,5},{5,4},{6,7},{7,6},{8,9},{9,8},{10,11... | collective-permute-start | bytes 1179656 | tf_op jit(solution)/shard_map/back0/ppermute | solution.py:327
  75.3 12.4 %collective-permute-start.20 = (f32[2,2,128,128]{3,2,1,0:T(8,128)S(1)}, f32[2,2,128,128]{3,2,1,0:T(8,128)S(1)}, u32[]{:S(2)}, u32[]{:S(2)}) collective-permute-start(f32[2,2,128,128]{3,2,1,0:T(8,128)S(1)} %get-tuple-element.170), channel_id=1, source_target_pairs={{0,1},{1,0},{2,3},{3,2},{4,5},{5,4},{6,7},{7,6},{8,9},{9,8},{10,11... | collective-permute-start | bytes 786440 | tf_op jit(solution)/shard_map/back2/ppermute | solution.py:327
  76.6 8.3 %collective-permute-start.17 = (f32[2,3,128,128]{3,2,1,0:T(8,128)S(1)}, f32[2,3,128,128]{3,2,1,0:T(8,128)S(1)}, u32[]{:S(2)}, u32[]{:S(2)}) collective-permute-start(f32[2,3,128,128]{3,2,1,0:T(8,128)S(1)} %get-tuple-element.163), channel_id=1, source_target_pairs={{0,4},{4,0},{1,5},{5,1},{2,6},{6,2},{3,7},{7,3},{8,12},{12,8},{9,1... | collective-permute-start | bytes 1179656 | tf_op jit(solution)/shard_map/core1/ppermute | solution.py:327
  85.1 11.1 %collective-permute-start.21 = (f32[2,3,128,128]{3,2,1,0:T(8,128)S(1)}, f32[2,3,128,128]{3,2,1,0:T(8,128)S(1)}, u32[]{:S(2)}, u32[]{:S(2)}) collective-permute-start(f32[2,3,128,128]{3,2,1,0:T(8,128)S(1)} %maximum_add_fusion.8), channel_id=1, source_target_pairs={{0,1},{1,0},{2,3},{3,2},{4,5},{5,4},{6,7},{7,6},{8,9},{9,8},{10,11... | collective-permute-start | bytes 1179656 | tf_op jit(solution)/shard_map/back1/ppermute | solution.py:327

commit v3 on v2

--- a/solution.py
+++ b/solution.py
@@ -10,18 +10,21 @@
 
 AXES = ("sa", "sb", "sc")
 CHUNKS = ((6, False), (6, False), (4, True))
-SPLIT = (2,)
+SPLIT = (0,)
 ORDER = (
     "pair0",
-    "inner1",
+    "mine1",
+    "theirs1",
     "pair2",
-    "inner0",
+    "plane2",
+    "mine0",
+    "found2",
+    "pair1",
+    "theirs0",
     "total0",
-    "plane2",
-    "pair1",
     "plane0",
-    "found2",
-    "inner2",
+    "mine2",
+    "theirs2",
     "state2",
     "total1",
     "plane1",
@@ -30,15 +33,15 @@
     "own0",
     "found1",
     "finish2",
+    "state1",
     "his0",
-    "state1",
     "own2",
     "his2",
     "own1",
     "his1",
 )
 SWAPS = (2, 1)
-COSTS = {'first': 100.0, 'load': 0.001, 'inner': 0.001, 'grads': 1000.0}
+COSTS = {'first': 100.0, 'load': 0.001, 'inner': 3000.0, 'grads': 1000.0}
 VMEM = 14 * 2**20
 ROWS = 128
 NN = (((1,), (0,)), ((), ()))
@@ -251,26 +254,26 @@
     return [[ref[i : i + size, place] for i in range(0, ref.shape[0], size)] for ref in refs]
 
 
-def inner_kernel(first, q_ref, k_ref, v_ref, g_ref, tie_ref, out_ref):
+def inner_kernel(place_ref, q_ref, k_ref, v_ref, g_ref, out_ref):
     size = ROWS
 
     @pl.loop(0, out_ref.shape[2] // size)
     def _(j):
-        for i, results in enumerate(inner_grads(*blocks_of((q_ref, k_ref, v_ref, g_ref), columns_at(first + j, size)))):
+        for i, results in enumerate(inner_grads(*blocks_of((q_ref, k_ref, v_ref, g_ref), columns_at(place_ref[0] + j, size)))):
             for n, x in enumerate(results):
                 out_ref[n, i * size : (i + 1) * size, columns_at(j, size)] = x
 
 
-def inner_terms(first, count, arrays, size, tie):
+def inner_terms(place, count, arrays, size):
     rows = arrays[0].shape[0]
     return call(
-        functools.partial(inner_kernel, first),
+        inner_kernel,
         pltpu.VMEM((3, rows, count * size), jnp.float32),
         IN_VMEM,
-        [IN_VMEM] * 4 + [ANYWHERE],
+        [IN_SMEM] + [IN_VMEM] * 4,
         COSTS["inner"] * count,
         "inner_terms",
-    )(*map(in_vmem, arrays), tie)
+    )(place, *map(in_vmem, arrays))
 
 
 def send_kernel(make, count, size, place_ref, outs, buffer, sems):
@@ -299,7 +302,7 @@
         before, after = state_ref[0, j], state_ref[1, j]
         for n, (ref, state) in enumerate(((g_ref, before.T), (v_ref, after), (k_ref, after.T))):
             x = fold(dot(wide(ref[:, place]), stacked(wide(state))))
-            x = x + inner_ref[n, :, columns_at(place_ref[1] + j, size)]
+            x = x + inner_ref[n, :, columns_at(j, size)]
             buffer[n, :, columns_at(j, size)] = (factor * x).astype(buffer.dtype)
 
     send_kernel(make, count, size, place_ref, outs, buffer, sems)
@@ -365,7 +368,7 @@
     faces = {k: (a ^ k) < a for k in range(1, sizes[0])}
     sides = jnp.stack([jnp.stack(own), jnp.stack(his)]).astype(jnp.int32)
     places = [
-        [jnp.stack([first[n], first[n] - starts[n]]).astype(jnp.int32) for n in chunks] for first in (own, his)
+        [first[n].astype(jnp.int32).reshape(1) for n in chunks] for first in (own, his)
     ]
     upper, pairs, chips, faces, sides, places = lax.optimization_barrier((upper, pairs, chips, faces, sides, places))
     order = Order()
@@ -439,12 +442,12 @@
             state[n, 0] = state[n, 0] + then(other)
         hand_back(n)
 
-    def inner(n):
-        inners[n] = did(inner_terms(starts[n], 2 * halves[n], arrays, size, order.last))
+    def inner(side, n):
+        inners[n, side] = did(inner_terms(then(places[side][n]), halves[n], arrays, size))
 
     def result(side, n):
         place = then(places[side][n])
-        outs[0] = grads(place, arrays, then(state[n, side]), inners[n], outs[0], factor)
+        outs[0] = grads(place, arrays, then(state[n, side]), inners[n, side], outs[0], factor)
         did(outs[0])
 
     steps = {
@@ -454,7 +457,8 @@
         "found": found_,
         "state": state_,
         "finish": finish,
-        "inner": inner,
+        "mine": functools.partial(inner, 0),
+        "theirs": functools.partial(inner, 1),
         "own": functools.partial(result, 0),
         "his": functools.partial(result, 1),
     }

time: 99.2 us -> 95.2 us (0.960)
  starting transfers between devices: 27.3 us -> 23.1 us
  waiting for transfers between devices: 20 us -> 23.5 us
  Pallas kernels: 48.7 us -> 45.4 us
    ppermute x22, starting transfers between devices: 27.3 us -> 23.1 us  [swap(): lax.ppermute(x, axis, [(i, i ^ offset) for i in range(lax.axis_size(axis))])]
    ppermute x22, waiting for transfers between devices: 20 us -> 23.5 us  [swap(): lax.ppermute(x, axis, [(i, i ^ offset) for i in range(lax.axis_size(axis))])]
    pallas_call x6, Pallas kernels: 15.8 us -> 12.5 us  [grads(): call(functools.partial(state_kernel, factor), [jax.ShapeDtypeStruct((rows...]
    pallas_call x3 -> x6, Pallas kernels: 21.9 us -> 21.9 us  [inner_terms(): call(inner_kernel, pltpu.VMEM((3, rows, count * size), jnp.float32), IN_V...]
  transfers between devices with their start and end apart: 22 -> 22, of which waited for: 9 -> 10; matrix products, arithmetic and copies ran while one was open for 2% -> 2% of each run, Pallas kernels for 43% -> 42%
where the time goes in v3:
time: 95.2 us; the launch traced here: 95 us
  Pallas kernels  45.4 us (48%)
  waiting for transfers between devices  23.5 us (25%)
  starting transfers between devices  23.1 us (24%)
  other arithmetic  1.85 us (2%)
  between operations  1.21 us (1%)
    ppermute x22, waiting for transfers between devices, swap(): lax.ppermute(x, axis, [(i, i ^ offset) for i in range(lax.axis_size(axis))])  23.5 us
    ppermute x22, starting transfers between devices, swap(): lax.ppermute(x, axis, [(i, i ^ offset) for i in range(lax.axis_size(axis))])  23.1 us
    pallas_call x6, Pallas kernels, inner_terms(): call(inner_kernel, pltpu.VMEM((3, rows, count * size), jnp.float32), IN_V...  21.9 us
    pallas_call x6, Pallas kernels, grads(): call(functools.partial(state_kernel, factor), [jax.ShapeDtypeStruct((rows...  12.5 us
    pallas_call x1, Pallas kernels, load_terms(): call(load_kernel, terms + terms[1:] + terms + [kept] * 4, [IN_VMEM] * (3...  8.06 us
    pallas_call x1, Pallas kernels, first_terms(): call(first_kernel, pltpu.VMEM((2, count, size, size), jnp.float32), IN_VM...  2.94 us
  transfers between devices with their start and end apart: 22, of which 10 were waited for; matrix products, arithmetic and copies ran while one was open for 2% of the time, Pallas kernels for 42%

profile of v3, /device:TPU:0, one launch (start us, length us, event | category | flops | bytes accessed | tf_op | source)
XLA Modules:
  0.0 95.0 jit_solution(6574129530179227431)
XLA Ops:
  0.8 2.9 %first_terms.1 = f32[2,3,128,128]{3,2,1,0:T(8,128)S(1)} custom-call(s32[2,3]{1,0:T(2,128)S(1)} %pad_add_fusion.place_ref, f32[512,2048]{1,0:T(8,128)} %q_ref.3, f32[512,2048]{1,0:T(8,128)} %k_ref.3, f32[512,2048]{1,0:T(8,128)} %v_ref.3, f32[512,2048]{1,0:T(8,128)} %g_ref.3), custom_call_target="tpu_custom_call" | custom-call | flops 100000000 | tf_op jit(solution)/shard_map/first_terms/pallas_call | solution.py:138
  3.7 3.1 %collective-permute-start.2 = (f32[2,3,128,128]{3,2,1,0:T(8,128)S(1)}, f32[2,3,128,128]{3,2,1,0:T(8,128)S(1)}, u32[]{:S(2)}, u32[]{:S(2)}) collective-permute-start(f32[2,3,128,128]{3,2,1,0:T(8,128)S(1)} %first_terms.1), channel_id=1, source_target_pairs={{0,1},{1,0},{2,3},{3,2},{4,5},{5,4},{6,7},{7,6},{8,9},{9,8},{10,11... | collective-permute-start | bytes 1179656 | tf_op jit(solution)/shard_map/swap0/ppermute | solution.py:330
  6.8 8.1 %load_terms.1 = (f32[2,3,128,128]{3,2,1,0:T(8,128)S(1)}, f32[2,3,128,128]{3,2,1,0:T(8,128)S(1)}, f32[2,2,128,128]{3,2,1,0:T(8,128)S(1)}, f32[2,3,128,128]{3,2,1,...) custom-call(s32[2,3]{1,0:T(2,128)S(1)} %pad_add_fusion.place_ref, ...), custom_call_target="tpu_custom_call" | custom-call | flops 1000 | tf_op jit(solution)/shard_map/load_terms/pallas_call | solution.py:201
  14.9 2.0 %collective-permute-start = (f32[2,3,128,128]{3,2,1,0:T(8,128)S(1)}, f32[2,3,128,128]{3,2,1,0:T(8,128)S(1)}, u32[]{:S(2)}, u32[]{:S(2)}) collective-permute-start(f32[2,3,128,128]{3,2,1,0:T(8,128)S(1)} %get-tuple-element.96), channel_id=1, source_target_pairs={{0,1},{1,0},{2,3},{3,2},{4,5},{5,4},{6,7},{7,6},{8,9},{9,8},{10,11... | collective-permute-start | bytes 1179656 | tf_op jit(solution)/shard_map/swap1/ppermute | solution.py:330
  17.1 2.7 %collective-permute-start.8 = (f32[2,3,128,128]{3,2,1,0:T(8,128)S(1)}, f32[2,3,128,128]{3,2,1,0:T(8,128)S(1)}, u32[]{:S(2)}, u32[]{:S(2)}) collective-permute-start(f32[2,3,128,128]{3,2,1,0:T(8,128)S(1)} %add.120), channel_id=1, source_target_pairs={{0,2},{1,3},{2,0},{3,1},{4,6},{5,7},{6,4},{7,5},{8,10},{9,11},{10,... | collective-permute-start | bytes 1179656 | tf_op jit(solution)/shard_map/middle0/ppermute | solution.py:330
  19.8 4.1 %inner_terms.6.inner_ref = f32[3,512,384]{2,1,0:T(8,128)S(1)} custom-call(s32[1]{0:T(128)} %bitcast.1.place_ref, f32[512,2048]{1,0:T(8,128)S(1)} %get-tuple-element.102.q_ref, f32[512,2048]{1,0:T(8,128)S(1)} %get-tuple-element.103.k_ref, f32[512,2048]{1,0:T(8,128)S(1)} %get-tuple-element.104.v_ref, f32[512,2048]{1,0:T(8,128)S(1)} %get-tuple-element.105.g_ref), custom_call_target="tpu_custom_call" | custom-call | flops 8999999488 | tf_op jit(solution)/shard_map/inner_terms/pallas_call | solution.py:269
  23.9 4.1 %inner_terms.7.inner_ref = f32[3,512,384]{2,1,0:T(8,128)S(1)} custom-call(s32[1]{0:T(128)} %bitcast.5.place_ref, f32[512,2048]{1,0:T(8,128)S(1)} %get-tuple-element.102.q_ref, f32[512,2048]{1,0:T(8,128)S(1)} %get-tuple-element.103.k_ref, f32[512,2048]{1,0:T(8,128)S(1)} %get-tuple-element.104.v_ref, f32[512,2048]{1,0:T(8,128)S(1)} %get-tuple-element.105.g_ref), custom_call_target="tpu_custom_call" | custom-call | flops 8999999488 | tf_op jit(solution)/shard_map/inner_terms/pallas_call | solution.py:269
  28.0 4.6 %collective-permute-done.1 = f32[2,2,128,128]{3,2,1,0:T(8,128)S(1)} collective-permute-done((f32[2,2,128,128]{3,2,1,0:T(8,128)S(1)}, f32[2,2,128,128]{3,2,1,0:T(8,128)S(1)}, u32[]{:S(2)}, u32[]{:S(2)}) %collective-permute-start.1) | collective-permute-done | bytes 262176 | tf_op jit(solution)/shard_map/swap2/ppermute | solution.py:330
  36.2 4.1 %inner_terms.8.inner_ref = f32[3,512,384]{2,1,0:T(8,128)S(1)} custom-call(s32[1]{0:T(128)} %bitcast.place_ref, f32[512,2048]{1,0:T(8,128)S(1)} %get-tuple-element.102.q_ref, f32[512,2048]{1,0:T(8,128)S(1)} %get-tuple-element.103.k_ref, f32[512,2048]{1,0:T(8,128)S(1)} %get-tuple-element.104.v_ref, f32[512,2048]{1,0:T(8,128)S(1)} %get-tuple-element.105.g_ref), custom_call_target="tpu_custom_call" | custom-call | flops 8999999488 | tf_op jit(solution)/shard_map/inner_terms/pallas_call | solution.py:269
  42.4 4.1 %inner_terms.9.inner_ref = f32[3,512,384]{2,1,0:T(8,128)S(1)} custom-call(s32[1]{0:T(128)} %bitcast.4.place_ref, f32[512,2048]{1,0:T(8,128)S(1)} %get-tuple-element.102.q_ref, f32[512,2048]{1,0:T(8,128)S(1)} %get-tuple-element.103.k_ref, f32[512,2048]{1,0:T(8,128)S(1)} %get-tuple-element.104.v_ref, f32[512,2048]{1,0:T(8,128)S(1)} %get-tuple-element.105.g_ref), custom_call_target="tpu_custom_call" | custom-call | flops 8999999488 | tf_op jit(solution)/shard_map/inner_terms/pallas_call | solution.py:269
  50.1 2.7 %inner_terms.10.inner_ref = f32[3,512,256]{2,1,0:T(8,128)S(1)} custom-call(s32[1]{0:T(128)} %bitcast.2.place_ref, f32[512,2048]{1,0:T(8,128)S(1)} %get-tuple-element.102.q_ref, f32[512,2048]{1,0:T(8,128)S(1)} %get-tuple-element.103.k_ref, f32[512,2048]{1,0:T(8,128)S(1)} %get-tuple-element.104.v_ref, f32[512,2048]{1,0:T(8,128)S(1)} %get-tuple-element.105.g_ref), custom_call_target="tpu_custom_call" | custom-call | flops 6000000000 | tf_op jit(solution)/shard_map/inner_terms/pallas_call | solution.py:269
  52.9 2.7 %inner_terms.11.inner_ref = f32[3,512,256]{2,1,0:T(8,128)S(1)} custom-call(s32[1]{0:T(128)} %bitcast.6.place_ref, f32[512,2048]{1,0:T(8,128)S(1)} %get-tuple-element.102.q_ref, f32[512,2048]{1,0:T(8,128)S(1)} %get-tuple-element.103.k_ref, f32[512,2048]{1,0:T(8,128)S(1)} %get-tuple-element.104.v_ref, f32[512,2048]{1,0:T(8,128)S(1)} %get-tuple-element.105.g_ref), custom_call_target="tpu_custom_call" | custom-call | flops 6000000000 | tf_op jit(solution)/shard_map/inner_terms/pallas_call | solution.py:269
  55.7 2.4 %collective-permute-start.18 = (f32[2,2,128,128]{3,2,1,0:T(8,128)S(1)}, f32[2,2,128,128]{3,2,1,0:T(8,128)S(1)}, u32[]{:S(2)}, u32[]{:S(2)}) collective-permute-start(f32[2,2,128,128]{3,2,1,0:T(8,128)S(1)} %get-tuple-element.173), channel_id=1, source_target_pairs={{0,2},{1,3},{2,0},{3,1},{4,6},{5,7},{6,4},{7,5},{8,10},{9,11},{10,... | collective-permute-start | bytes 786440 | tf_op jit(solution)/shard_map/middle2/ppermute | solution.py:330
  60.4 1.7 %collective-permute-start.16 = (f32[3,128,128]{2,1,0:T(8,128)S(1)}, f32[3,128,128]{2,1,0:T(8,128)S(1)}, u32[]{:S(2)}, u32[]{:S(2)}) collective-permute-start(f32[3,128,128]{2,1,0:T(8,128)S(1)} %get-tuple-element.192), channel_id=1, source_target_pairs={{0,24},{8,16},{16,8},{24,0},{1,25},{9,17},{17,9},{25,1},{2,26},{10... | collective-permute-start | bytes 589832 | tf_op jit(solution)/shard_map/plane1/ppermute | solution.py:330
  64.7 2.2 %state_grads.6 = (bf16[512,2048]{1,0:T(8,128)(2,1)}, bf16[512,2048]{1,0:T(8,128)(2,1)}, bf16[512,2048]{1,0:T(8,128)(2,1)}) custom-call(s32[1]{0:T(128)} %bitcast.place_ref, f32[512,2048]{1,0:T(8,128)S(1)} %get-tuple-element.103.k_ref, f32[512,2048]{1,0:T(8,128)S(1)} %get-tuple-element.104.v_ref, f32[512,2048]{1,0:T(8,128)S(1)} %get-tuple-element.105.g_ref, ...), custom_call_target="tpu_custom_call" | custom-call | flops 3000000000 | tf_op jit(solution)/shard_map/state_grads/pallas_call | solution.py:316
  66.9 4.0 %collective-permute-done.16 = f32[3,128,128]{2,1,0:T(8,128)S(1)} collective-permute-done((f32[3,128,128]{2,1,0:T(8,128)S(1)}, f32[3,128,128]{2,1,0:T(8,128)S(1)}, u32[]{:S(2)}, u32[]{:S(2)}) %collective-permute-start.16) | collective-permute-done | bytes 196640 | tf_op jit(solution)/shard_map/plane1/ppermute | solution.py:330
  71.0 3.5 %collective-permute-done.15 = f32[3,128,128]{2,1,0:T(8,128)S(1)} collective-permute-done((f32[3,128,128]{2,1,0:T(8,128)S(1)}, f32[3,128,128]{2,1,0:T(8,128)S(1)}, u32[]{:S(2)}, u32[]{:S(2)}) %collective-permute-start.15) | collective-permute-done | bytes 196640 | tf_op jit(solution)/shard_map/plane1/ppermute | solution.py:330
  78.7 2.2 %state_grads.7 = (bf16[512,2048]{1,0:T(8,128)(2,1)}, bf16[512,2048]{1,0:T(8,128)(2,1)}, bf16[512,2048]{1,0:T(8,128)(2,1)}) custom-call(s32[1]{0:T(128)} %bitcast.4.place_ref, f32[512,2048]{1,0:T(8,128)S(1)} %get-tuple-element.103.k_ref, f32[512,2048]{1,0:T(8,128)S(1)} %get-tuple-element.104.v_ref, ...), custom_call_target="tpu_custom_call", output_to_operand_aliasing={{0}: (6, {}), {1}: (7, {}), {2}: (8, {})} | custom-call | flops 3000000000 | tf_op jit(solution)/shard_map/state_grads/pallas_call | solution.py:316
  80.9 1.8 %state_grads.8 = (bf16[512,2048]{1,0:T(8,128)(2,1)}, bf16[512,2048]{1,0:T(8,128)(2,1)}, bf16[512,2048]{1,0:T(8,128)(2,1)}) custom-call(s32[1]{0:T(128)} %bitcast.2.place_ref, f32[512,2048]{1,0:T(8,128)S(1)} %get-tuple-element.103.k_ref, f32[512,2048]{1,0:T(8,128)S(1)} %get-tuple-element.104.v_ref, ...), custom_call_target="tpu_custom_call", output_to_operand_aliasing={{0}: (6, {}), {1}: (7, {}), {2}: (8, {})} | custom-call | flops 2000000000 | tf_op jit(solution)/shard_map/state_grads/pallas_call | solution.py:316
  82.7 1.6 %collective-permute-done.20.state_ref = f32[2,2,128,128]{3,2,1,0:T(8,128)S(1)} collective-permute-done((f32[2,2,128,128]{3,2,1,0:T(8,128)S(1)}, f32[2,2,128,128]{3,2,1,0:T(8,128)S(1)}, u32[]{:S(2)}, u32[]{:S(2)}) %collective-permute-start.20) | collective-permute-done | bytes 262176 | tf_op jit(solution)/shard_map/back2/ppermute | solution.py:330
  84.3 1.8 %state_grads.9 = (bf16[512,2048]{1,0:T(8,128)(2,1)}, bf16[512,2048]{1,0:T(8,128)(2,1)}, bf16[512,2048]{1,0:T(8,128)(2,1)}) custom-call(s32[1]{0:T(128)} %bitcast.6.place_ref, f32[512,2048]{1,0:T(8,128)S(1)} %get-tuple-element.103.k_ref, f32[512,2048]{1,0:T(8,128)S(1)} %get-tuple-element.104.v_ref, ...), custom_call_target="tpu_custom_call", output_to_operand_aliasing={{0}: (6, {}), {1}: (7, {}), {2}: (8, {})} | custom-call | flops 2000000000 | tf_op jit(solution)/shard_map/state_grads/pallas_call | solution.py:316
  86.0 2.3 %state_grads.10 = (bf16[512,2048]{1,0:T(8,128)(2,1)}, bf16[512,2048]{1,0:T(8,128)(2,1)}, bf16[512,2048]{1,0:T(8,128)(2,1)}) custom-call(s32[1]{0:T(128)} %bitcast.1.place_ref, f32[512,2048]{1,0:T(8,128)S(1)} %get-tuple-element.103.k_ref, f32[512,2048]{1,0:T(8,128)S(1)} %get-tuple-element.104.v_ref, ...), custom_call_target="tpu_custom_call", output_to_operand_aliasing={{0}: (6, {}), {1}: (7, {}), {2}: (8, {})} | custom-call | flops 3000000000 | tf_op jit(solution)/shard_map/state_grads/pallas_call | solution.py:316
  88.3 4.3 %collective-permute-done.21.state_ref = f32[2,3,128,128]{3,2,1,0:T(8,128)S(1)} collective-permute-done((f32[2,3,128,128]{3,2,1,0:T(8,128)S(1)}, f32[2,3,128,128]{3,2,1,0:T(8,128)S(1)}, u32[]{:S(2)}, u32[]{:S(2)}) %collective-permute-start.21) | collective-permute-done | bytes 393248 | tf_op jit(solution)/shard_map/back1/ppermute | solution.py:330
  92.6 2.2 %state_grads.11 = (bf16[512,2048]{1,0:T(8,128)(2,1)}, bf16[512,2048]{1,0:T(8,128)(2,1)}, bf16[512,2048]{1,0:T(8,128)(2,1)}) custom-call(s32[1]{0:T(128)} %bitcast.5.place_ref, f32[512,2048]{1,0:T(8,128)S(1)} %get-tuple-element.103.k_ref, f32[512,2048]{1,0:T(8,128)S(1)} %get-tuple-element.104.v_ref, ...), custom_call_target="tpu_custom_call", output_to_operand_aliasing={{0}: (6, {}), {1}: (7, {}), {2}: (8, {})} | custom-call | flops 3000000000 | tf_op jit(solution)/shard_map/state_grads/pallas_call | solution.py:316
  (73 shorter events, 18.5 us)
Async XLA Ops:
  3.7 13.4 %collective-permute-start.2 = (f32[2,3,128,128]{3,2,1,0:T(8,128)S(1)}, f32[2,3,128,128]{3,2,1,0:T(8,128)S(1)}, u32[]{:S(2)}, u32[]{:S(2)}) collective-permute-start(f32[2,3,128,128]{3,2,1,0:T(8,128)S(1)} %first_terms.1), channel_id=1, source_target_pairs={{0,1},{1,0},{2,3},{3,2},{4,5},{5,4},{6,7},{7,6},{8,9},{9,8},{10,11... | collective-permute-start | bytes 1179656 | tf_op jit(solution)/shard_map/swap0/ppermute | solution.py:330
  14.9 17.7 %collective-permute-start.1 = (f32[2,2,128,128]{3,2,1,0:T(8,128)S(1)}, f32[2,2,128,128]{3,2,1,0:T(8,128)S(1)}, u32[]{:S(2)}, u32[]{:S(2)}) collective-permute-start(f32[2,2,128,128]{3,2,1,0:T(8,128)S(1)} %get-tuple-element.98), channel_id=1, source_target_pairs={{0,1},{1,0},{2,3},{3,2},{4,5},{5,4},{6,7},{7,6},{8,9},{9,8},{10,11... | collective-permute-start | bytes 786440 | tf_op jit(solution)/shard_map/swap2/ppermute | solution.py:330
  14.9 26.7 %collective-permute-start = (f32[2,3,128,128]{3,2,1,0:T(8,128)S(1)}, f32[2,3,128,128]{3,2,1,0:T(8,128)S(1)}, u32[]{:S(2)}, u32[]{:S(2)}) collective-permute-start(f32[2,3,128,128]{3,2,1,0:T(8,128)S(1)} %get-tuple-element.96), channel_id=1, source_target_pairs={{0,1},{1,0},{2,3},{3,2},{4,5},{5,4},{6,7},{7,6},{8,9},{9,8},{10,11... | collective-permute-start | bytes 1179656 | tf_op jit(solution)/shard_map/swap1/ppermute | solution.py:330
  17.1 29.3 %collective-permute-start.8 = (f32[2,3,128,128]{3,2,1,0:T(8,128)S(1)}, f32[2,3,128,128]{3,2,1,0:T(8,128)S(1)}, u32[]{:S(2)}, u32[]{:S(2)}) collective-permute-start(f32[2,3,128,128]{3,2,1,0:T(8,128)S(1)} %add.120), channel_id=1, source_target_pairs={{0,2},{1,3},{2,0},{3,1},{4,6},{5,7},{6,4},{7,5},{8,10},{9,11},{10,... | collective-permute-start | bytes 1179656 | tf_op jit(solution)/shard_map/middle0/ppermute | solution.py:330
  32.7 8.8 %collective-permute-start.3 = (f32[2,128,128]{2,1,0:T(8,128)S(1)}, f32[2,128,128]{2,1,0:T(8,128)S(1)}, u32[]{:S(2)}, u32[]{:S(2)}) collective-permute-start(f32[2,128,128]{2,1,0:T(8,128)S(1)} %get-tuple-element.207), channel_id=1, source_target_pairs={{0,8},{8,0},{16,24},{24,16},{1,9},{9,1},{17,25},{25,17},{2,10},{10... | collective-permute-start | bytes 393224 | tf_op jit(solution)/shard_map/plane2/ppermute | solution.py:330
  34.2 7.3 %collective-permute-start.5 = (f32[2,128,128]{2,1,0:T(8,128)S(1)}, f32[2,128,128]{2,1,0:T(8,128)S(1)}, u32[]{:S(2)}, u32[]{:S(2)}) collective-permute-start(f32[2,128,128]{2,1,0:T(8,128)S(1)} %get-tuple-element.208), channel_id=1, source_target_pairs={{0,24},{8,16},{16,8},{24,0},{1,25},{9,17},{17,9},{25,1},{2,26},{10... | collective-permute-start | bytes 393224 | tf_op jit(solution)/shard_map/plane2/ppermute | solution.py:330
  35.7 5.8 %collective-permute-start.4 = (f32[2,128,128]{2,1,0:T(8,128)S(1)}, f32[2,128,128]{2,1,0:T(8,128)S(1)}, u32[]{:S(2)}, u32[]{:S(2)}) collective-permute-start(f32[2,128,128]{2,1,0:T(8,128)S(1)} %get-tuple-element.209), channel_id=1, source_target_pairs={{0,16},{8,24},{16,0},{24,8},{1,17},{9,25},{17,1},{25,9},{2,18},{10... | collective-permute-start | bytes 393224 | tf_op jit(solution)/shard_map/plane2/ppermute | solution.py:330
  41.7 17.0 %collective-permute-start.6 = (f32[2,3,128,128]{3,2,1,0:T(8,128)S(1)}, f32[2,3,128,128]{3,2,1,0:T(8,128)S(1)}, u32[]{:S(2)}, u32[]{:S(2)}) collective-permute-start(f32[2,3,128,128]{3,2,1,0:T(8,128)S(1)} %add.124), channel_id=1, source_target_pairs={{0,2},{1,3},{2,0},{3,1},{4,6},{5,7},{6,4},{7,5},{8,10},{9,11},{10,... | collective-permute-start | bytes 1179656 | tf_op jit(solution)/shard_map/middle1/ppermute | solution.py:330
  42.4 13.3 %collective-permute-start.7 = (f32[2,2,128,128]{3,2,1,0:T(8,128)S(1)}, f32[2,2,128,128]{3,2,1,0:T(8,128)S(1)}, u32[]{:S(2)}, u32[]{:S(2)}) collective-permute-start(f32[2,2,128,128]{3,2,1,0:T(8,128)S(1)} %get-tuple-element.179), channel_id=1, source_target_pairs={{0,4},{4,0},{1,5},{5,1},{2,6},{6,2},{3,7},{7,3},{8,12},{12,8},{9,1... | collective-permute-start | bytes 786440 | tf_op jit(solution)/shard_map/core2/ppermute | solution.py:330
  46.6 13.9 %collective-permute-start.12 = (f32[3,128,128]{2,1,0:T(8,128)S(1)}, f32[3,128,128]{2,1,0:T(8,128)S(1)}, u32[]{:S(2)}, u32[]{:S(2)}) collective-permute-start(f32[3,128,128]{2,1,0:T(8,128)S(1)} %get-tuple-element.200), channel_id=1, source_target_pairs={{0,24},{8,16},{16,8},{24,0},{1,25},{9,17},{17,9},{25,1},{2,26},{10... | collective-permute-start | bytes 589832 | tf_op jit(solution)/shard_map/plane0/ppermute | solution.py:330
  48.1 14.0 %collective-permute-start.10 = (f32[3,128,128]{2,1,0:T(8,128)S(1)}, f32[3,128,128]{2,1,0:T(8,128)S(1)}, u32[]{:S(2)}, u32[]{:S(2)}) collective-permute-start(f32[3,128,128]{2,1,0:T(8,128)S(1)} %get-tuple-element.201), channel_id=1, source_target_pairs={{0,8},{8,0},{16,24},{24,16},{1,9},{9,1},{17,25},{25,17},{2,10},{10... | collective-permute-start | bytes 589832 | tf_op jit(solution)/shard_map/plane0/ppermute | solution.py:330
  49.2 12.9 %collective-permute-start.11 = (f32[3,128,128]{2,1,0:T(8,128)S(1)}, f32[3,128,128]{2,1,0:T(8,128)S(1)}, u32[]{:S(2)}, u32[]{:S(2)}) collective-permute-start(f32[3,128,128]{2,1,0:T(8,128)S(1)} %get-tuple-element.202), channel_id=1, source_target_pairs={{0,16},{8,24},{16,0},{24,8},{1,17},{9,25},{17,1},{25,9},{2,18},{10... | collective-permute-start | bytes 589832 | tf_op jit(solution)/shard_map/plane0/ppermute | solution.py:330
  55.7 19.0 %collective-permute-start.18 = (f32[2,2,128,128]{3,2,1,0:T(8,128)S(1)}, f32[2,2,128,128]{3,2,1,0:T(8,128)S(1)}, u32[]{:S(2)}, u32[]{:S(2)}) collective-permute-start(f32[2,2,128,128]{3,2,1,0:T(8,128)S(1)} %get-tuple-element.173), channel_id=1, source_target_pairs={{0,2},{1,3},{2,0},{3,1},{4,6},{5,7},{6,4},{7,5},{8,10},{9,11},{10,... | collective-permute-start | bytes 786440 | tf_op jit(solution)/shard_map/middle2/ppermute | solution.py:330
  58.8 15.6 %collective-permute-start.9 = (f32[3,128,128]{2,1,0:T(8,128)S(1)}, f32[3,128,128]{2,1,0:T(8,128)S(1)}, u32[]{:S(2)}, u32[]{:S(2)}) collective-permute-start(f32[3,128,128]{2,1,0:T(8,128)S(1)} %get-tuple-element.191), channel_id=1, source_target_pairs={{0,8},{8,0},{16,24},{24,16},{1,9},{9,1},{17,25},{25,17},{2,10},{10... | collective-permute-start | bytes 589832 | tf_op jit(solution)/shard_map/plane1/ppermute | solution.py:330
  60.4 10.5 %collective-permute-start.16 = (f32[3,128,128]{2,1,0:T(8,128)S(1)}, f32[3,128,128]{2,1,0:T(8,128)S(1)}, u32[]{:S(2)}, u32[]{:S(2)}) collective-permute-start(f32[3,128,128]{2,1,0:T(8,128)S(1)} %get-tuple-element.192), channel_id=1, source_target_pairs={{0,24},{8,16},{16,8},{24,0},{1,25},{9,17},{17,9},{25,1},{2,26},{10... | collective-permute-start | bytes 589832 | tf_op jit(solution)/shard_map/plane1/ppermute | solution.py:330
  62.4 1.5 %collective-permute-start.13 = (f32[3,128,128]{2,1,0:T(8,128)S(1)}, f32[3,128,128]{2,1,0:T(8,128)S(1)}, u32[]{:S(2)}, u32[]{:S(2)}) collective-permute-start(f32[3,128,128]{2,1,0:T(8,128)S(1)} %get-tuple-element.183), channel_id=1, source_target_pairs={{0,4},{4,0},{1,5},{5,1},{2,6},{6,2},{3,7},{7,3},{8,12},{12,8},{9,1... | collective-permute-start | bytes 589832 | tf_op jit(solution)/shard_map/core0/ppermute | solution.py:330
  62.5 1.8 %collective-permute-start.14 = (f32[3,128,128]{2,1,0:T(8,128)S(1)}, f32[3,128,128]{2,1,0:T(8,128)S(1)}, u32[]{:S(2)}, u32[]{:S(2)}) collective-permute-start(f32[3,128,128]{2,1,0:T(8,128)S(1)} %get-tuple-element.184), channel_id=1, source_target_pairs={{0,4},{4,0},{1,5},{5,1},{2,6},{6,2},{3,7},{7,3},{8,12},{12,8},{9,1... | collective-permute-start | bytes 589832 | tf_op jit(solution)/shard_map/core0/ppermute | solution.py:330
  63.9 10.6 %collective-permute-start.15 = (f32[3,128,128]{2,1,0:T(8,128)S(1)}, f32[3,128,128]{2,1,0:T(8,128)S(1)}, u32[]{:S(2)}, u32[]{:S(2)}) collective-permute-start(f32[3,128,128]{2,1,0:T(8,128)S(1)} %get-tuple-element.193), channel_id=1, source_target_pairs={{0,16},{8,24},{16,0},{24,8},{1,17},{9,25},{17,1},{25,9},{2,18},{10... | collective-permute-start | bytes 589832 | tf_op jit(solution)/shard_map/plane1/ppermute | solution.py:330
  64.5 14.2 %collective-permute-start.19 = (f32[2,3,128,128]{3,2,1,0:T(8,128)S(1)}, f32[2,3,128,128]{3,2,1,0:T(8,128)S(1)}, u32[]{:S(2)}, u32[]{:S(2)}) collective-permute-start(f32[2,3,128,128]{3,2,1,0:T(8,128)S(1)} %maximum_add_fusion.3), channel_id=1, source_target_pairs={{0,1},{1,0},{2,3},{3,2},{4,5},{5,4},{6,7},{7,6},{8,9},{9,8},{10,11... | collective-permute-start | bytes 1179656 | tf_op jit(solution)/shard_map/back0/ppermute | solution.py:330
  74.8 1.8 %collective-permute-start.17 = (f32[2,3,128,128]{3,2,1,0:T(8,128)S(1)}, f32[2,3,128,128]{3,2,1,0:T(8,128)S(1)}, u32[]{:S(2)}, u32[]{:S(2)}) collective-permute-start(f32[2,3,128,128]{3,2,1,0:T(8,128)S(1)} %get-tuple-element.175), channel_id=1, source_target_pairs={{0,4},{4,0},{1,5},{5,1},{2,6},{6,2},{3,7},{7,3},{8,12},{12,8},{9,1... | collective-permute-start | bytes 1179656 | tf_op jit(solution)/shard_map/core1/ppermute | solution.py:330
  74.9 9.3 %collective-permute-start.20 = (f32[2,2,128,128]{3,2,1,0:T(8,128)S(1)}, f32[2,2,128,128]{3,2,1,0:T(8,128)S(1)}, u32[]{:S(2)}, u32[]{:S(2)}) collective-permute-start(f32[2,2,128,128]{3,2,1,0:T(8,128)S(1)} %get-tuple-element.182), channel_id=1, source_target_pairs={{0,1},{1,0},{2,3},{3,2},{4,5},{5,4},{6,7},{7,6},{8,9},{9,8},{10,11... | collective-permute-start | bytes 786440 | tf_op jit(solution)/shard_map/back2/ppermute | solution.py:330
  76.7 15.9 %collective-permute-start.21 = (f32[2,3,128,128]{3,2,1,0:T(8,128)S(1)}, f32[2,3,128,128]{3,2,1,0:T(8,128)S(1)}, u32[]{:S(2)}, u32[]{:S(2)}) collective-permute-start(f32[2,3,128,128]{3,2,1,0:T(8,128)S(1)} %maximum_add_fusion.8), channel_id=1, source_target_pairs={{0,1},{1,0},{2,3},{3,2},{4,5},{5,4},{6,7},{7,6},{8,9},{9,8},{10,11... | collective-permute-start | bytes 1179656 | tf_op jit(solution)/shard_map/back1/ppermute | solution.py:330
